TPU v7x, 128 devices: a whole 4x4x4 slice. The times are simulated.
128 devices in a mesh: row: 8 (over z_lo, y), col: 16 (over z_hi, x, core).
Axes of the slice: x: 4, y: 4, z: 4 (z_hi: 2, z_lo: 2; z = z_hi * 2 + z_lo), core: 2. Of those that a mesh axis runs over, the one named last changes fastest.
Arguments:
- object_field: float32 [2, 2048, 4096], P(None, 'row', 'col'), may hold values from -6 to 6
- probe_modes: float32 [4, 2, 256, 256], replicated, may hold values from -3 to 3
- positions: int32 [8, 16, 6, 2], P('row', 'col'), may hold values from 0 to 255
- counts: int32 [8, 16], P('row', 'col'), may hold values from 0 to 6, as said below
- amplitude: float32 [8, 16, 6, 256, 256], P('row', 'col'), may hold values from 0 to 2
Outputs:
- updated: float32 [2, 2048, 4096], P(None, 'row', 'col')
Inputs may be any that keep to these rules, and one draw needn't show every extreme that they name: The counts of two tiles in one tile row whose column indices differ by 8 add up to 6; some tile has exactly 6. Only positions below a tile's count are used.
All inputs are finite; a program needn't handle non-finite values.
Results may differ from a plain program's by a relative error of at most 0.0018.
Values sent between devices are 32-bit elements; how exact they have to be, the bound alone decides.
No kernel may reach another device: no remote copies, remote signals or barrier semaphores. Data moves between devices by JAX's collectives and lax.ppermute only.
A program may use at most 64 MiB of HBM per device.

v0:
```python
import math

import jax
import jax.numpy as jnp
from jax import lax
from jax.sharding import PartitionSpec as P

ITERS = 2


step_size = 0.1
damping = 0.1


def from_behind(block, axis, distance):
    devices = range(lax.axis_size(axis))
    route = [(i - distance, i) for i in devices if i - distance in devices]
    return lax.ppermute(block, axis, route)


def blocks(upper_left, upper_right, lower_left, lower_right):
    return jnp.stack(
        [
            jnp.stack([upper_left, upper_right], axis=1),
            jnp.stack([lower_left, lower_right], axis=1),
        ],
        axis=0,
    )


def tables(width):
    ladder = jnp.arange(width, dtype=jnp.int32)
    product = ladder[:, None] * ladder[None, :] % width
    theta = product.astype(jnp.float32) * (2.0 * math.pi / width)
    factor = 1.0 / math.sqrt(width)
    cosine = jnp.cos(theta) * factor
    minus_sine = -jnp.sin(theta) * factor
    table_fwd = blocks(cosine, -minus_sine, minus_sine, cosine).astype(jnp.bfloat16)
    table_inv = blocks(cosine, minus_sine, -minus_sine, cosine).astype(jnp.bfloat16)
    return (table_fwd, table_inv)


def patch_gradient(patch, measured, probe_modes, table_fwd, table_inv):
    probe_re = probe_modes[:, 0]
    probe_im = probe_modes[:, 1]
    psi = jnp.stack(
        [probe_re * patch[0] - probe_im * patch[1], probe_re * patch[1] + probe_im * patch[0]],
        axis=1,
    ).astype(jnp.bfloat16)
    section = jnp.einsum(
        "cjdk,mdkl->mcjl", table_fwd, psi, preferred_element_type=jnp.float32
    ).astype(jnp.bfloat16)
    far = jnp.einsum("mcjk,ckdl->mdjl", section, table_inv, preferred_element_type=jnp.float32)
    intensity = jnp.sum(far * far, axis=(0, 1))
    ratio = 1.0 - measured / jnp.sqrt(intensity + damping)
    chi = (far * ratio).astype(jnp.bfloat16)
    back = jnp.einsum("cjdk,mdkl->mcjl", table_inv, chi, preferred_element_type=jnp.float32).astype(
        jnp.bfloat16
    )
    wave = jnp.einsum("mcjk,ckdl->mdjl", back, table_fwd, preferred_element_type=jnp.float32)
    grad_re = jnp.sum(probe_re * wave[:, 0] + probe_im * wave[:, 1], axis=0)
    grad_im = jnp.sum(probe_re * wave[:, 1] - probe_im * wave[:, 0], axis=0)
    return jnp.stack([grad_re, grad_im], axis=0)


def body(object_field, probe_modes, positions, counts, amplitude):
    width = probe_modes.shape[-1]
    tile = object_field.shape[1]
    table_fwd, table_inv = tables(width)
    count = counts[0, 0]
    offsets = positions[0, 0]
    measured_all = amplitude[0, 0]
    most = measured_all.shape[0]
    anchor = jnp.int32(0)
    field = object_field
    for sweep in range(ITERS):
        below = from_behind(field, "row", -1)
        column = jnp.concatenate([field, below], axis=1)
        beside = from_behind(column, "col", -1)
        extended = jnp.concatenate([column, beside], axis=2)

        def cut(slot):
            return lax.dynamic_slice(
                extended, (anchor, offsets[slot, 0], offsets[slot, 1]), (2, width, width)
            )

        patches = lax.map(cut, jnp.arange(most, dtype=jnp.int32))
        grads = lax.map(
            lambda pair: patch_gradient(pair[0], pair[1], probe_modes, table_fwd, table_inv),
            (patches, measured_all),
        )
        live = jnp.arange(most, dtype=jnp.int32) < count
        slot_grads = jnp.where(live[:, None, None, None], grads, 0.0)

        def place(slot, total):
            top = offsets[slot, 0]
            left = offsets[slot, 1]
            current = lax.dynamic_slice(total, (anchor, top, left), (2, width, width))
            return lax.dynamic_update_slice(total, current + slot_grads[slot], (anchor, top, left))

        total = lax.fori_loop(0, most, place, jnp.zeros_like(extended))
        from_left = from_behind(total[:, :, tile:], "col", 1)
        column_sum = total[:, :, :tile] + from_left
        from_above = from_behind(column_sum[:, tile:], "row", 1)
        field = field - step_size * (column_sum[:, :tile] + from_above)
    return field


def solution(mesh):
    placed = (
        P(None, "row", "col"),
        P(),
        P("row", "col", None, None),
        P("row", "col"),
        P("row", "col", None, None, None),
    )
    return jax.shard_map(
        body, mesh=mesh, in_specs=placed, out_specs=P(None, "row", "col"), check_vma=False
    )
```

profile of v0, /device:TPU:96, one launch (start us, length us, event | category | flops | bytes accessed | tf_op | source)
XLA Modules:
  0.0 575.2 jit_solution(4063260977761838383)
XLA Ops:
  5.8 10.4 %collective-permute-done = f32[2,256,256]{2,1,0:T(8,128)S(1)} collective-permute-done((f32[2,256,256]{2,1,0:T(8,128)}, f32[2,256,256]{2,1,0:T(8,128)S(1)}, u32[]{:S(2)}, u32[]{:S(2)}) %collective-permute-start) | collective-permute-done | bytes 524320 | tf_op jit(solution)/shard_map/ppermute | solution.py:18
  23.8 7.7 %collective-permute-done.1 = f32[2,512,256]{2,1,0:T(8,128)} collective-permute-done((f32[2,512,256]{2,1,0:T(8,128)S(1)}, f32[2,512,256]{2,1,0:T(8,128)}, u32[]{:S(2)}, u32[]{:S(2)}) %collective-permute-start.1) | collective-permute-done | bytes 1048608 | tf_op jit(solution)/shard_map/ppermute | solution.py:18
  35.0 46.9 %while.66 = (s32[]{:T(128)}, f32[6,2,256,256]{3,2,1,0:T(8,128)}, s32[6]{0:T(128)S(1)}, s32[6,2]{0,1:T(2,128)S(1)}, f32[2,512,512]{2,1,0:T(8,128)S(1)}, /*index=5*/s32[]{:T(128)}, s32[]{:T(128)}, s32[]{:T(128)}, s32[]{:T(128)}) while((s32[]{:T(128)}, f32[6,2,256,256]{3,2,1,0:T(8,128)}, s32[6]{0:T(128)S(1)}, s32[6,2]{0,1:T(2,128)S(1)}, ...), condition=%wide.region_1.2_spmd, body=%wide.region_0.1_spmd.sunk | while | flops 11 | bytes 1049323 | solution.py:87
  84.2 81.5 %while.67 = (s32[]{:T(128)}, f32[6,2,256,256]{3,2,1,0:T(8,128)}, f32[4,2,256,256]{3,2,1,0:T(8,128)S(1)}, f32[6,2,256,256]{3,2,1,0:T(8,128)}, bf16[2,256,2,256]{3...) while((s32[]{:T(128)}, f32[6,2,256,256]{3,2,1,0:T(8,128)}, ...), condition=%wide.region_6.7_spmd, body=%wide.region_2.6_spmd.sunk | while | flops 2157051904 | bytes 21234300 | solution.py:88
  171.3 75.1 %while.68 = (s32[]{:T(128)}, f32[2,512,512]{2,1,0:T(8,128)}, s32[6,2]{0,1:T(2,128)S(1)}, f32[6,2,256,256]{3,2,1,0:T(8,128)}, s32[]{:T(128)}, /*index=5*/s32[]{:T(128)}, s32[]{:T(128)}) while((s32[]{:T(128)}, f32[2,512,512]{2,1,0:T(8,128)}, s32[6,2]{0,1:T(2,128)S(1)}, f32[6,2,256,256]{3,2,1,0:T(8,128)}, s32[]{:T(128)}, /*index=5*/s32[]{:T(128)}, ...), condition=%wide.region_8.9_spmd, body=%wide.region_7.8_spmd.sunk | while | flops 131080 | bytes 2621621 | solution.py:101
  177.2 6.6 %dynamic_update_slice.39 = f32[2,512,512]{2,1,0:T(8,128)} dynamic-update-slice(f32[2,512,512]{2,1,0:T(8,128)} %get-tuple-element.718, f32[2,256,256]{2,1,0:T(8,128)S(1)} %bitcast_add_fusion.4, s32[]{:T(128)} %constant.128.clone.1..sunk.2, s32[]{:T(128)S(6)} %select_n.138, s32[]{:T(128)S(6)} %select_n.139) | dynamic-update-slice | bytes 1048580 | tf_op jit(solution)/shard_map/while/body/eval_jaxpr/dynamic_update_slice | solution.py:99
  189.7 6.8 %dynamic_update_slice.39 = f32[2,512,512]{2,1,0:T(8,128)} dynamic-update-slice(f32[2,512,512]{2,1,0:T(8,128)} %get-tuple-element.718, f32[2,256,256]{2,1,0:T(8,128)S(1)} %bitcast_add_fusion.4, s32[]{:T(128)} %constant.128.clone.1..sunk.2, s32[]{:T(128)S(6)} %select_n.138, s32[]{:T(128)S(6)} %select_n.139) | dynamic-update-slice | bytes 1048580 | tf_op jit(solution)/shard_map/while/body/eval_jaxpr/dynamic_update_slice | solution.py:99
  202.4 6.6 %dynamic_update_slice.39 = f32[2,512,512]{2,1,0:T(8,128)} dynamic-update-slice(f32[2,512,512]{2,1,0:T(8,128)} %get-tuple-element.718, f32[2,256,256]{2,1,0:T(8,128)S(1)} %bitcast_add_fusion.4, s32[]{:T(128)} %constant.128.clone.1..sunk.2, s32[]{:T(128)S(6)} %select_n.138, s32[]{:T(128)S(6)} %select_n.139) | dynamic-update-slice | bytes 1048580 | tf_op jit(solution)/shard_map/while/body/eval_jaxpr/dynamic_update_slice | solution.py:99
  214.9 6.6 %dynamic_update_slice.39 = f32[2,512,512]{2,1,0:T(8,128)} dynamic-update-slice(f32[2,512,512]{2,1,0:T(8,128)} %get-tuple-element.718, f32[2,256,256]{2,1,0:T(8,128)S(1)} %bitcast_add_fusion.4, s32[]{:T(128)} %constant.128.clone.1..sunk.2, s32[]{:T(128)S(6)} %select_n.138, s32[]{:T(128)S(6)} %select_n.139) | dynamic-update-slice | bytes 1048580 | tf_op jit(solution)/shard_map/while/body/eval_jaxpr/dynamic_update_slice | solution.py:99
  227.4 6.8 %dynamic_update_slice.39 = f32[2,512,512]{2,1,0:T(8,128)} dynamic-update-slice(f32[2,512,512]{2,1,0:T(8,128)} %get-tuple-element.718, f32[2,256,256]{2,1,0:T(8,128)S(1)} %bitcast_add_fusion.4, s32[]{:T(128)} %constant.128.clone.1..sunk.2, s32[]{:T(128)S(6)} %select_n.138, s32[]{:T(128)S(6)} %select_n.139) | dynamic-update-slice | bytes 1048580 | tf_op jit(solution)/shard_map/while/body/eval_jaxpr/dynamic_update_slice | solution.py:99
  250.1 17.6 %collective-permute-done.2 = f32[2,512,256]{2,1,0:T(8,128)S(1)} collective-permute-done((f32[2,512,256]{2,1,0:T(8,128)S(1)}, f32[2,512,256]{2,1,0:T(8,128)S(1)}, u32[]{:S(2)}, u32[]{:S(2)}) %collective-permute-start.2) | collective-permute-done | bytes 1048608 | tf_op jit(solution)/shard_map/ppermute | solution.py:18
  271.2 9.9 %collective-permute-done.3 = f32[2,256,256]{2,1,0:T(8,128)S(1)} collective-permute-done((f32[2,256,256]{2,1,0:T(8,128)S(1)}, f32[2,256,256]{2,1,0:T(8,128)S(1)}, u32[]{:S(2)}, u32[]{:S(2)}) %collective-permute-start.3) | collective-permute-done | bytes 524320 | tf_op jit(solution)/shard_map/ppermute | solution.py:18
  284.2 8.1 %collective-permute-done.4 = f32[2,256,256]{2,1,0:T(8,128)S(1)} collective-permute-done((f32[2,256,256]{2,1,0:T(8,128)S(1)}, f32[2,256,256]{2,1,0:T(8,128)S(1)}, u32[]{:S(2)}, u32[]{:S(2)}) %collective-permute-start.4) | collective-permute-done | bytes 524320 | tf_op jit(solution)/shard_map/ppermute | solution.py:18
  293.4 8.9 %collective-permute-start.5 = (f32[2,512,256]{2,1,0:T(8,128)}, f32[2,512,256]{2,1,0:T(8,128)}, u32[]{:S(2)}, u32[]{:S(2)}) collective-permute-start(f32[2,512,256]{2,1,0:T(8,128)} %pad_maximum_fusion.2), channel_id=1, source_target_pairs={{1,0},{2,1},{3,2},{4,3},{5,4},{6,5},{7,6},{8,7},{9,8},{10,9},{11,1... | collective-permute-start | bytes 3145736 | tf_op jit(solution)/shard_map/ppermute | solution.py:18
  302.3 12.4 %collective-permute-done.5 = f32[2,512,256]{2,1,0:T(8,128)} collective-permute-done((f32[2,512,256]{2,1,0:T(8,128)}, f32[2,512,256]{2,1,0:T(8,128)}, u32[]{:S(2)}, u32[]{:S(2)}) %collective-permute-start.5) | collective-permute-done | bytes 1048608 | tf_op jit(solution)/shard_map/ppermute | solution.py:18
  319.5 55.7 %while.69 = (s32[]{:T(128)}, f32[6,2,256,256]{3,2,1,0:T(8,128)}, s32[6]{0:T(128)S(1)}, s32[6,2]{0,1:T(2,128)S(1)}, f32[2,512,512]{2,1,0:T(8,128)}, /*index=5*/s32[]{:T(128)}, s32[]{:T(128)}, s32[]{:T(128)}, s32[]{:T(128)}) while((s32[]{:T(128)}, f32[6,2,256,256]{3,2,1,0:T(8,128)}, s32[6]{0:T(128)S(1)}, s32[6,2]{0,1:T(2,128)S(1)}, ...), condition=%wide.region_10.11_spmd, body=%wide.region_9.10_spmd.sunk | while | flops 11 | bytes 1049323 | solution.py:87
  377.2 81.5 %while.70 = (s32[]{:T(128)}, f32[6,2,256,256]{3,2,1,0:T(8,128)}, f32[4,2,256,256]{3,2,1,0:T(8,128)S(1)}, f32[6,2,256,256]{3,2,1,0:T(8,128)}, bf16[2,256,2,256]{3...) while((s32[]{:T(128)}, f32[6,2,256,256]{3,2,1,0:T(8,128)}, ...), condition=%wide.region_15.16_spmd, body=%wide.region_11.15_spmd.sunk | while | flops 2157051904 | bytes 21234300 | solution.py:88
  464.3 75.3 %while.71 = (s32[]{:T(128)}, f32[2,512,512]{2,1,0:T(8,128)}, s32[6,2]{0,1:T(2,128)S(1)}, f32[6,2,256,256]{3,2,1,0:T(8,128)}, s32[]{:T(128)}, /*index=5*/s32[]{:T(128)}, s32[]{:T(128)}) while((s32[]{:T(128)}, f32[2,512,512]{2,1,0:T(8,128)}, s32[6,2]{0,1:T(2,128)S(1)}, f32[6,2,256,256]{3,2,1,0:T(8,128)}, s32[]{:T(128)}, ...), condition=%wide.region_17.18_spmd, body=%wide.region_16.17_spmd.sunk | while | flops 131080 | bytes 2621621 | solution.py:101
  470.2 6.6 %dynamic_update_slice.42 = f32[2,512,512]{2,1,0:T(8,128)} dynamic-update-slice(f32[2,512,512]{2,1,0:T(8,128)} %get-tuple-element.796, f32[2,256,256]{2,1,0:T(8,128)S(1)} %bitcast_add_fusion.5, s32[]{:T(128)} %constant.128.clone.1..sunk.5, s32[]{:T(128)S(6)} %select_n.143, s32[]{:T(128)S(6)} %select_n.144) | dynamic-update-slice | bytes 1048580 | tf_op jit(solution)/shard_map/while/body/eval_jaxpr/dynamic_update_slice | solution.py:99
  482.8 6.8 %dynamic_update_slice.42 = f32[2,512,512]{2,1,0:T(8,128)} dynamic-update-slice(f32[2,512,512]{2,1,0:T(8,128)} %get-tuple-element.796, f32[2,256,256]{2,1,0:T(8,128)S(1)} %bitcast_add_fusion.5, s32[]{:T(128)} %constant.128.clone.1..sunk.5, s32[]{:T(128)S(6)} %select_n.143, s32[]{:T(128)S(6)} %select_n.144) | dynamic-update-slice | bytes 1048580 | tf_op jit(solution)/shard_map/while/body/eval_jaxpr/dynamic_update_slice | solution.py:99
  495.5 6.6 %dynamic_update_slice.42 = f32[2,512,512]{2,1,0:T(8,128)} dynamic-update-slice(f32[2,512,512]{2,1,0:T(8,128)} %get-tuple-element.796, f32[2,256,256]{2,1,0:T(8,128)S(1)} %bitcast_add_fusion.5, s32[]{:T(128)} %constant.128.clone.1..sunk.5, s32[]{:T(128)S(6)} %select_n.143, s32[]{:T(128)S(6)} %select_n.144) | dynamic-update-slice | bytes 1048580 | tf_op jit(solution)/shard_map/while/body/eval_jaxpr/dynamic_update_slice | solution.py:99
  520.5 6.8 %dynamic_update_slice.42 = f32[2,512,512]{2,1,0:T(8,128)} dynamic-update-slice(f32[2,512,512]{2,1,0:T(8,128)} %get-tuple-element.796, f32[2,256,256]{2,1,0:T(8,128)S(1)} %bitcast_add_fusion.5, s32[]{:T(128)} %constant.128.clone.1..sunk.5, s32[]{:T(128)S(6)} %select_n.143, s32[]{:T(128)S(6)} %select_n.144) | dynamic-update-slice | bytes 1048580 | tf_op jit(solution)/shard_map/while/body/eval_jaxpr/dynamic_update_slice | solution.py:99
  543.1 17.8 %collective-permute-done.6 = f32[2,512,256]{2,1,0:T(8,128)S(1)} collective-permute-done((f32[2,512,256]{2,1,0:T(8,128)S(1)}, f32[2,512,256]{2,1,0:T(8,128)S(1)}, u32[]{:S(2)}, u32[]{:S(2)}) %collective-permute-start.6) | collective-permute-done | bytes 1048608 | tf_op jit(solution)/shard_map/ppermute | solution.py:18
  563.1 11.3 %collective-permute-done.7 = f32[2,256,256]{2,1,0:T(8,128)S(1)} collective-permute-done((f32[2,256,256]{2,1,0:T(8,128)S(1)}, f32[2,256,256]{2,1,0:T(8,128)S(1)}, u32[]{:S(2)}, u32[]{:S(2)}) %collective-permute-start.7) | collective-permute-done | bytes 524320 | tf_op jit(solution)/shard_map/ppermute | solution.py:18
  (198 shorter events, 296.9 us)
Async XLA Ops:
  0.0 16.2 %collective-permute-start = (f32[2,256,256]{2,1,0:T(8,128)}, f32[2,256,256]{2,1,0:T(8,128)S(1)}, u32[]{:S(2)}, u32[]{:S(2)}) collective-permute-start(f32[2,256,256]{2,1,0:T(8,128)} %param.17), channel_id=1, source_target_pairs={{16,0},{32,16},{48,32},{64,48},{80,64},{96,80},{112,96},{17,1},{33... | collective-permute-start | bytes 1572872 | tf_op jit(solution)/shard_map/ppermute | solution.py:18
  16.3 15.2 %collective-permute-start.1 = (f32[2,512,256]{2,1,0:T(8,128)S(1)}, f32[2,512,256]{2,1,0:T(8,128)}, u32[]{:S(2)}, u32[]{:S(2)}) collective-permute-start(f32[2,512,256]{2,1,0:T(8,128)S(1)} %constant_dynamic-update-slice_fusion), channel_id=1, source_target_pairs={{1,0},{2,1},{3,2},{4,3},{5,4},{6,5},{7,6},{8,7},{9,8},{10,9},{11,1... | collective-permute-start | bytes 3145736 | tf_op jit(solution)/shard_map/ppermute | solution.py:18
  33.0 2.0 copy-start.6
  81.9 2.3 copy-start
  246.4 21.3 %copy-start.2 = (f32[2,512,512]{2,1,0:T(8,128)S(1)}, f32[2,512,512]{2,1,0:T(8,128)}, u32[]{:S(2)}) copy-start(f32[2,512,512]{2,1,0:T(8,128)} %get-tuple-element.293) | copy-start | bytes 6291460
  247.8 33.3 %copy-start.5 = (f32[2,256,256]{2,1,0:T(8,128)S(1)}, f32[2,256,256]{2,1,0:T(8,128)}, u32[]{:S(2)}) copy-start(f32[2,256,256]{2,1,0:T(8,128)} %param.17) | copy-start | bytes 1572868
  247.8 19.9 %collective-permute-start.2 = (f32[2,512,256]{2,1,0:T(8,128)S(1)}, f32[2,512,256]{2,1,0:T(8,128)S(1)}, u32[]{:S(2)}, u32[]{:S(2)}) collective-permute-start(f32[2,512,256]{2,1,0:T(8,128)S(1)} %slice.73), channel_id=1, source_target_pairs={{0,1},{1,2},{2,3},{3,4},{4,5},{5,6},{6,7},{7,8},{8,9},{9,10},{10,1... | collective-permute-start | bytes 3145736 | tf_op jit(solution)/shard_map/ppermute | solution.py:18
  267.9 13.2 %collective-permute-start.3 = (f32[2,256,256]{2,1,0:T(8,128)S(1)}, f32[2,256,256]{2,1,0:T(8,128)S(1)}, u32[]{:S(2)}, u32[]{:S(2)}) collective-permute-start(f32[2,256,256]{2,1,0:T(8,128)S(1)} %slice.85), channel_id=1, source_target_pairs={{0,16},{16,32},{32,48},{48,64},{64,80},{80,96},{96,112},{1,17},{17... | collective-permute-start | bytes 1572872 | tf_op jit(solution)/shard_map/ppermute | solution.py:18
  281.2 36.3 %copy-start.3 = (f32[2,256,256]{2,1,0:T(8,128)}, f32[2,256,256]{2,1,0:T(8,128)S(1)}, u32[]{:S(2)}) copy-start(f32[2,256,256]{2,1,0:T(8,128)S(1)} %fusion.59) | copy-start | bytes 1572868
  281.3 11.1 %collective-permute-start.4 = (f32[2,256,256]{2,1,0:T(8,128)S(1)}, f32[2,256,256]{2,1,0:T(8,128)S(1)}, u32[]{:S(2)}, u32[]{:S(2)}) collective-permute-start(f32[2,256,256]{2,1,0:T(8,128)S(1)} %fusion.59), channel_id=1, source_target_pairs={{16,0},{32,16},{48,32},{64,48},{80,64},{96,80},{112,96},{17,1},{33... | collective-permute-start | bytes 1572872 | tf_op jit(solution)/shard_map/ppermute | solution.py:18
  293.4 21.3 %collective-permute-start.5 = (f32[2,512,256]{2,1,0:T(8,128)}, f32[2,512,256]{2,1,0:T(8,128)}, u32[]{:S(2)}, u32[]{:S(2)}) collective-permute-start(f32[2,512,256]{2,1,0:T(8,128)} %pad_maximum_fusion.2), channel_id=1, source_target_pairs={{1,0},{2,1},{3,2},{4,3},{5,4},{6,5},{7,6},{8,7},{9,8},{10,9},{11,1... | collective-permute-start | bytes 3145736 | tf_op jit(solution)/shard_map/ppermute | solution.py:18
  539.6 21.3 %copy-start.1 = (f32[2,512,512]{2,1,0:T(8,128)S(1)}, f32[2,512,512]{2,1,0:T(8,128)}, u32[]{:S(2)}) copy-start(f32[2,512,512]{2,1,0:T(8,128)} %get-tuple-element.296) | copy-start | bytes 6291460
  541.0 33.3 %copy-start.4 = (f32[2,256,256]{2,1,0:T(8,128)S(1)}, f32[2,256,256]{2,1,0:T(8,128)}, u32[]{:S(2)}) copy-start(f32[2,256,256]{2,1,0:T(8,128)} %copy-done.3) | copy-start | bytes 1572868
  541.0 19.9 %collective-permute-start.6 = (f32[2,512,256]{2,1,0:T(8,128)S(1)}, f32[2,512,256]{2,1,0:T(8,128)S(1)}, u32[]{:S(2)}, u32[]{:S(2)}) collective-permute-start(f32[2,512,256]{2,1,0:T(8,128)S(1)} %slice.77), channel_id=1, source_target_pairs={{0,1},{1,2},{2,3},{3,4},{4,5},{5,6},{6,7},{7,8},{8,9},{9,10},{10,1... | collective-permute-start | bytes 3145736 | tf_op jit(solution)/shard_map/ppermute | solution.py:18
  561.1 13.2 %collective-permute-start.7 = (f32[2,256,256]{2,1,0:T(8,128)S(1)}, f32[2,256,256]{2,1,0:T(8,128)S(1)}, u32[]{:S(2)}, u32[]{:S(2)}) collective-permute-start(f32[2,256,256]{2,1,0:T(8,128)S(1)} %slice.87), channel_id=1, source_target_pairs={{0,16},{16,32},{32,48},{48,64},{64,80},{80,96},{96,112},{1,17},{17... | collective-permute-start | bytes 1572872 | tf_op jit(solution)/shard_map/ppermute | solution.py:18
where the time goes:
time: 582 us; the launch traced here: 575 us
  local copies, waits for them, and re-layouts  151 us (26%)
  loops' own time  113 us (19%)
  matrix products  101 us (17%)
  waiting for transfers between devices  95.2 us (16%)
  other arithmetic  85.3 us (15%)
  starting transfers between devices  29 us (5%)
    ppermute x8, waiting for transfers between devices, from_behind(): return lax.ppermute(block, axis, route)  95.2 us
    dynamic_update_slice x12, local copies, waits for them, and re-layouts, place(): lax.dynamic_update_slice(total, current + slot_grads[slot], (anchor, top,...  79.3 us
    another operation x2, loops' own time, body(): patches = lax.map(cut, jnp.arange(most, dtype=jnp.int32))  67.7 us
    dot_general x12, matrix products, patch_gradient(): jnp.einsum('mcjk,ckdl->mdjl', back, table_fwd, preferred_element_type=jnp...  54.1 us
    dot_general x12, matrix products, patch_gradient(): jnp.einsum('mcjk,ckdl->mdjl', section, table_inv, preferred_element_type=...  46.8 us
    another operation x2, loops' own time, body(): total = lax.fori_loop(0, most, place, jnp.zeros_like(extended))  45.3 us
    ppermute x8, starting transfers between devices, from_behind(): return lax.ppermute(block, axis, route)  29 us
    reduce_sum x12, other arithmetic, patch_gradient(): grad_re = jnp.sum(probe_re * wave[:, 0] + probe_im * wave[:, 1], axis=0)  23.6 us
  transfers between devices with their start and end apart: 8, of which 8 were waited for; matrix products, arithmetic and copies ran while one was open for 1% of the time, Pallas kernels for 0%

commit v1 on v0

v1 whole, which is shorter than its diff:
```python
import math

import jax
import jax.numpy as jnp
import ml_dtypes
import numpy as np
from jax import lax
from jax.experimental import pallas as pl
from jax.experimental.pallas import tpu as pltpu
from jax.sharding import PartitionSpec as P

ITERS = 2
STEP = 0.1
DAMPING = 0.1
SIDE = 256
HALF = 128
F32 = jnp.float32
BF16 = jnp.bfloat16
VMEM = pl.BlockSpec(memory_space=pltpu.VMEM)
SMEM = pl.BlockSpec(memory_space=pltpu.SMEM)


def from_behind(block, axis, distance):
    devices = range(lax.axis_size(axis))
    route = [(i - distance, i) for i in devices if i - distance in devices]
    return lax.ppermute(block, axis, route)


def tables():
    ladder = np.arange(SIDE, dtype=np.int32)
    theta = (ladder[:, None] * ladder[None, :] % SIDE).astype(np.float32)
    theta = theta * np.float32(2.0 * math.pi / SIDE)
    factor = np.float32(1.0 / math.sqrt(SIDE))
    cosine, sine = np.cos(theta) * factor, np.sin(theta) * factor
    forms = []
    for parity in (0, 1):
        c, s = cosine[parity::2, :HALF], sine[parity::2, :HALF]
        forms.append(np.block([[c, s], [-s, c]]))
    forms += [f.T for f in forms]
    return np.stack(forms).astype(ml_dtypes.bfloat16)


def parity_order():
    order = np.concatenate([np.arange(0, SIDE, 2), np.arange(1, SIDE, 2)])
    matrix = np.zeros((SIDE, SIDE), np.float32)
    matrix[order, np.arange(SIDE)] = 1.0
    return matrix


def sort_kernel(order_ref, flip_ref, amp_ref, out_ref):
    exact = dict(preferred_element_type=F32, precision=lax.Precision.HIGHEST)
    wide = jnp.dot(amp_ref[0], order_ref[...], **exact)
    out_ref[0] = jnp.dot(flip_ref[...], wide, **exact)


def sort_amplitude(amplitude):
    most = amplitude.shape[0]
    order = parity_order()
    whole = pl.BlockSpec((SIDE, SIDE), lambda s: (0, 0))
    one = pl.BlockSpec((1, SIDE, SIDE), lambda s: (s, 0, 0))
    return pl.pallas_call(
        sort_kernel,
        grid=(most,),
        out_shape=jax.ShapeDtypeStruct(amplitude.shape, F32),
        in_specs=[whole, whole, one],
        out_specs=one,
        cost_estimate=pl.CostEstimate(
            flops=most * 24 * SIDE**3, bytes_accessed=8 * amplitude.size, transcendentals=0
        ),
    )(order, np.ascontiguousarray(order.T), amplitude)


def dot(a, b):
    return jnp.dot(a, b, preferred_element_type=F32)


def lanes(a, b):
    return jnp.concatenate([a, b], axis=1)


def rows(a, b):
    return jnp.concatenate([a, b], axis=0)


def update_kernel(
    offsets_ref,
    count_ref,
    own_ref,
    below_ref,
    right_ref,
    diag_ref,
    probe_ref,
    amp_ref,
    table_ref,
    own_out,
    below_out,
    right_out,
    diag_out,
    patch,
    far,
    level,
    grad,
):
    modes = probe_ref.shape[0]
    outs = (own_out, below_out, right_out, diag_out)
    for out in outs:
        out[...] = jnp.zeros_like(out)
    row = lax.broadcasted_iota(jnp.int32, (SIDE, SIDE), 0)
    column = lax.broadcasted_iota(jnp.int32, (SIDE, SIDE), 1)

    def position(slot, _):
        top, left = offsets_ref[slot, 0], offsets_ref[slot, 1]
        here, beside = row >= top, column >= left
        for part in (0, 1):
            mixed = jnp.where(
                here,
                jnp.where(beside, own_ref[part], right_ref[part]),
                jnp.where(beside, below_ref[part], diag_ref[part]),
            )
            mixed = pltpu.roll(mixed, lax.rem(SIDE - left, SIDE), 1)
            patch[part] = pltpu.roll(mixed, lax.rem(SIDE - top, SIDE), 0)
        for m in range(modes):
            sums, differences = [], []
            psi = []
            for half in (0, 1):
                at = pl.ds(half * HALF, HALF)
                pr, pi = probe_ref[m, 0, at, :], probe_ref[m, 1, at, :]
                xr, xi = patch[0, at, :], patch[1, at, :]
                psi.append(rows(pr * xr - pi * xi, pr * xi + pi * xr))
            even = dot(table_ref[0], (psi[0] + psi[1]).astype(BF16))
            odd = dot(table_ref[1], (psi[0] - psi[1]).astype(BF16))
            for s in (even, odd):
                a, b = s[:, :HALF], s[:, HALF:]
                u, v = (a + b).astype(BF16), (a - b).astype(BF16)
                sums.append(lanes(u[:HALF], u[HALF:]))
                differences.append(lanes(v[:HALF], v[HALF:]))
            for q, block in ((0, rows(*sums)), (1, rows(*differences))):
                f = dot(block, table_ref[2 + q])
                far[m, q] = f
                power = f[:, :HALF] * f[:, :HALF] + f[:, HALF:] * f[:, HALF:]
                at = pl.ds(q * HALF, HALF)
                if m:
                    power = power + level[:, at]
                level[:, at] = power
        level[...] = 1.0 - amp_ref[slot] / jnp.sqrt(level[...] + DAMPING)
        for m in range(modes):
            chi = []
            for q in (0, 1):
                ratio = level[:, q * HALF : (q + 1) * HALF]
                chi.append((far[m, q] * lanes(ratio, ratio)).astype(BF16))
            halves = []
            for parity in (0, 1):
                c = [x[parity * HALF : (parity + 1) * HALF] for x in chi]
                real = lanes(c[0][:, :HALF], c[1][:, :HALF])
                imag = lanes(c[0][:, HALF:], c[1][:, HALF:])
                halves.append(dot(table_ref[2 + parity], rows(real, imag)))
            top_back = (halves[0] + halves[1]).astype(BF16)
            bottom_back = (halves[0] - halves[1]).astype(BF16)
            wave = []
            for q in (0, 1):
                at = slice(q * HALF, (q + 1) * HALF)
                block = rows(
                    lanes(top_back[:HALF, at], top_back[HALF:, at]),
                    lanes(bottom_back[:HALF, at], bottom_back[HALF:, at]),
                )
                wave.append(dot(block, table_ref[q]))
            for side, w in ((0, wave[0] + wave[1]), (1, wave[0] - wave[1])):
                at = pl.ds(side * HALF, HALF)
                pr, pi = probe_ref[m, 0, :, at], probe_ref[m, 1, :, at]
                wr, wi = w[:, :HALF], w[:, HALF:]
                gr, gi = pr * wr + pi * wi, pr * wi - pi * wr
                if m:
                    gr, gi = gr + grad[0, :, at], gi + grad[1, :, at]
                grad[0, :, at] = gr
                grad[1, :, at] = gi
        for part in (0, 1):
            turned = pltpu.roll(pltpu.roll(grad[part], top, 0), left, 1)
            upper, lower = jnp.where(here, turned, 0.0), jnp.where(here, 0.0, turned)
            own_out[part] += jnp.where(beside, upper, 0.0)
            right_out[part] += jnp.where(beside, 0.0, upper)
            below_out[part] += jnp.where(beside, lower, 0.0)
            diag_out[part] += jnp.where(beside, 0.0, lower)
        return 0

    lax.fori_loop(0, count_ref[0], position, 0)


def gradient(offsets, count, own, below, right, diag, probe, amplitude, table):
    modes = probe.shape[0]
    tile = (2, SIDE, SIDE)
    return pl.pallas_call(
        update_kernel,
        out_shape=[jax.ShapeDtypeStruct(tile, F32)] * 4,
        in_specs=[SMEM, SMEM] + [VMEM] * 7,
        out_specs=[VMEM] * 4,
        scratch_shapes=[
            pltpu.VMEM(tile, F32),
            pltpu.VMEM((modes, 2, SIDE, SIDE), F32),
            pltpu.VMEM((SIDE, SIDE), F32),
            pltpu.VMEM(tile, F32),
        ],
        compiler_params=pltpu.CompilerParams(vmem_limit_bytes=48 * 2**20),
    )(offsets, count, own, below, right, diag, probe, amplitude, table)


def body(object_field, probe_modes, positions, counts, amplitude):
    table = tables()
    count = counts[0]
    offsets = positions[0, 0]
    sorted_amp = sort_amplitude(amplitude[0, 0])
    field = object_field
    for sweep in range(ITERS):
        below = from_behind(field, "row", -1)
        right = from_behind(field, "col", -1)
        diag = from_behind(below, "col", -1)
        own_sum, below_sum, right_sum, diag_sum = gradient(
            offsets, count, field, below, right, diag, probe_modes, sorted_amp, table
        )
        below_sum = below_sum + from_behind(diag_sum, "col", 1)
        total = own_sum + from_behind(right_sum, "col", 1) + from_behind(below_sum, "row", 1)
        field = field - STEP * total
    return field


def solution(mesh):
    placed = (
        P(None, "row", "col"),
        P(),
        P("row", "col", None, None),
        P("row", "col"),
        P("row", "col", None, None, None),
    )
    return jax.shard_map(
        body, mesh=mesh, in_specs=placed, out_specs=P(None, "row", "col"), check_vma=False
    )
```

time: 582 us -> 155 us (0.27)
  the two profiles are of different devices: /device:TPU:96 before, /device:TPU:101 now
where the time goes in v1:
time: 155 us
  waiting for transfers between devices  76 us (49%)
  Pallas kernels  46.5 us (30%)
  starting transfers between devices  30 us (19%)
    ppermute x12, waiting for transfers between devices, from_behind(): return lax.ppermute(block, axis, route)  76 us
    pallas_call x2, Pallas kernels, gradient(): pl.pallas_call(update_kernel, out_shape=[jax.ShapeDtypeStruct(tile, F32)]...  38 us
    ppermute x12, starting transfers between devices, from_behind(): return lax.ppermute(block, axis, route)  30 us
    pallas_call x1, Pallas kernels, sort_amplitude(): pl.pallas_call(sort_kernel, grid=(most,), out_shape=jax.ShapeDtypeStruct(...  8.48 us
  transfers between devices with their start and end apart: 12, of which 11 were waited for; matrix products, arithmetic and copies ran while one was open for 1% of the time, Pallas kernels for 5%

profile of v1, /device:TPU:101, one launch (start us, length us, event | category | flops | bytes accessed | tf_op | source)
XLA Modules:
  0.0 155.3 jit_solution(7881781722791907384)
XLA Ops:
  0.0 4.5 %collective-permute-start = (f32[2,256,256]{2,1,0:T(8,128)}, f32[2,256,256]{2,1,0:T(8,128)S(1)}, u32[]{:S(2)}, u32[]{:S(2)}) collective-permute-start(f32[2,256,256]{2,1,0:T(8,128)} %own_ref.1), channel_id=1, source_target_pairs={{16,0},{32,16},{48,32},{64,48},{80,64},{96,80},{112,96},{17,1},{33... | collective-permute-start | bytes 1572872 | tf_op jit(solution)/shard_map/ppermute | solution.py:26
  4.5 2.9 %collective-permute-start.1 = (f32[2,256,256]{2,1,0:T(8,128)}, f32[2,256,256]{2,1,0:T(8,128)S(1)}, u32[]{:S(2)}, u32[]{:S(2)}) collective-permute-start(f32[2,256,256]{2,1,0:T(8,128)} %own_ref.1), channel_id=1, source_target_pairs={{1,0},{2,1},{3,2},{4,3},{5,4},{6,5},{7,6},{8,7},{9,8},{10,9},{11,1... | collective-permute-start | bytes 1572872 | tf_op jit(solution)/shard_map/ppermute | solution.py:26
  7.4 8.0 %collective-permute-done.below_ref = f32[2,256,256]{2,1,0:T(8,128)S(1)} collective-permute-done((f32[2,256,256]{2,1,0:T(8,128)}, f32[2,256,256]{2,1,0:T(8,128)S(1)}, u32[]{:S(2)}, u32[]{:S(2)}) %collective-permute-start) | collective-permute-done | bytes 524320 | tf_op jit(solution)/shard_map/ppermute | solution.py:26
  15.4 3.4 %collective-permute-start.2 = (f32[2,256,256]{2,1,0:T(8,128)S(1)}, f32[2,256,256]{2,1,0:T(8,128)S(1)}, u32[]{:S(2)}, u32[]{:S(2)}) collective-permute-start(f32[2,256,256]{2,1,0:T(8,128)S(1)} %collective-permute-done.below_ref), channel_id=1, source_target_pairs={{1,0},{2,1},{3,2},{4,3},{5,4},{6,5},{7,6},{8,7},{9,8},{10,9},{11,1... | collective-permute-start | bytes 1572872 | tf_op jit(solution)/shard_map/ppermute | solution.py:26
  20.2 8.5 %shard_map.82.amp_ref = f32[6,256,256]{2,1,0:T(8,128)} custom-call(f32[256,256]{1,0:T(8,128)} %constant.8.clone.order_ref, f32[256,256]{1,0:T(8,128)} %constant.9.clone.flip_ref, f32[6,256,256]{2,1,0:T(8,128)} %bitcast.6), custom_call_target="tpu_custom_call" | custom-call | flops 2415919104 | bytes 3145728 | tf_op jit(solution)/shard_map/pallas_call | solution.py:61
  28.7 3.3 %collective-permute-done.2.diag_ref = f32[2,256,256]{2,1,0:T(8,128)S(1)} collective-permute-done((f32[2,256,256]{2,1,0:T(8,128)S(1)}, f32[2,256,256]{2,1,0:T(8,128)S(1)}, u32[]{:S(2)}, u32[]{:S(2)}) %collective-permute-start.2) | collective-permute-done | bytes 524320 | tf_op jit(solution)/shard_map/ppermute | solution.py:26
  32.0 19.0 %shard_map.83 = (f32[2,256,256]{2,1,0:T(8,128)S(1)}, f32[2,256,256]{2,1,0:T(8,128)S(1)}, f32[2,256,256]{2,1,0:T(8,128)S(1)}, f32[2,256,256]{2,1,0:T(8,128)S(1)}) custom-call(s32[6,2]{1,0:T(8,128)S(1)} %copy.9.offsets_ref, s32[1]{0:T(128)} %bitcast.3.count_ref, f32[2,256,256]{2,1,0:T(8,128)S(1)} %copy-done, ...), custom_call_target="tpu_custom_call" | custom-call | tf_op jit(solution)/shard_map/pallas_call | solution.py:191
  51.0 1.9 %collective-permute-start.4 = (f32[2,256,256]{2,1,0:T(8,128)S(1)}, f32[2,256,256]{2,1,0:T(8,128)S(1)}, u32[]{:S(2)}, u32[]{:S(2)}) collective-permute-start(f32[2,256,256]{2,1,0:T(8,128)S(1)} %get-tuple-element.16), channel_id=1, source_target_pairs={{0,1},{1,2},{2,3},{3,4},{4,5},{5,6},{6,7},{7,8},{8,9},{9,10},{10,1... | collective-permute-start | bytes 1572872 | tf_op jit(solution)/shard_map/ppermute | solution.py:26
  53.0 2.1 %collective-permute-start.3 = (f32[2,256,256]{2,1,0:T(8,128)S(1)}, f32[2,256,256]{2,1,0:T(8,128)S(1)}, u32[]{:S(2)}, u32[]{:S(2)}) collective-permute-start(f32[2,256,256]{2,1,0:T(8,128)S(1)} %get-tuple-element.14), channel_id=1, source_target_pairs={{0,1},{1,2},{2,3},{3,4},{4,5},{5,6},{6,7},{7,8},{8,9},{9,10},{10,1... | collective-permute-start | bytes 1572872 | tf_op jit(solution)/shard_map/ppermute | solution.py:26
  55.1 4.0 %collective-permute-done.4 = f32[2,256,256]{2,1,0:T(8,128)S(1)} collective-permute-done((f32[2,256,256]{2,1,0:T(8,128)S(1)}, f32[2,256,256]{2,1,0:T(8,128)S(1)}, u32[]{:S(2)}, u32[]{:S(2)}) %collective-permute-start.4) | collective-permute-done | bytes 524320 | tf_op jit(solution)/shard_map/ppermute | solution.py:26
  59.1 1.9 %collective-permute-start.5 = (f32[2,256,256]{2,1,0:T(8,128)S(1)}, f32[2,256,256]{2,1,0:T(8,128)S(1)}, u32[]{:S(2)}, u32[]{:S(2)}) collective-permute-start(f32[2,256,256]{2,1,0:T(8,128)S(1)} %add.19), channel_id=1, source_target_pairs={{0,16},{16,32},{32,48},{48,64},{64,80},{80,96},{96,112},{1,17},{17... | collective-permute-start | bytes 1572872 | tf_op jit(solution)/shard_map/ppermute | solution.py:26
  61.1 3.6 %collective-permute-done.3 = f32[2,256,256]{2,1,0:T(8,128)S(1)} collective-permute-done((f32[2,256,256]{2,1,0:T(8,128)S(1)}, f32[2,256,256]{2,1,0:T(8,128)S(1)}, u32[]{:S(2)}, u32[]{:S(2)}) %collective-permute-start.3) | collective-permute-done | bytes 524320 | tf_op jit(solution)/shard_map/ppermute | solution.py:26
  64.7 17.9 %collective-permute-done.5 = f32[2,256,256]{2,1,0:T(8,128)S(1)} collective-permute-done((f32[2,256,256]{2,1,0:T(8,128)S(1)}, f32[2,256,256]{2,1,0:T(8,128)S(1)}, u32[]{:S(2)}, u32[]{:S(2)}) %collective-permute-start.5) | collective-permute-done | bytes 524320 | tf_op jit(solution)/shard_map/ppermute | solution.py:26
  82.7 3.6 %collective-permute-start.6 = (f32[2,256,256]{2,1,0:T(8,128)S(1)}, f32[2,256,256]{2,1,0:T(8,128)S(1)}, u32[]{:S(2)}, u32[]{:S(2)}) collective-permute-start(f32[2,256,256]{2,1,0:T(8,128)S(1)} %multiply_subtract_fusion.1.own_ref), channel_id=1, source_target_pairs={{16,0},{32,16},{48,32},{64,48},{80,64},{96,80},{112,96},{17,1},{33... | collective-permute-start | bytes 1572872 | tf_op jit(solution)/shard_map/ppermute | solution.py:26
  86.4 1.9 %collective-permute-start.7 = (f32[2,256,256]{2,1,0:T(8,128)S(1)}, f32[2,256,256]{2,1,0:T(8,128)S(1)}, u32[]{:S(2)}, u32[]{:S(2)}) collective-permute-start(f32[2,256,256]{2,1,0:T(8,128)S(1)} %multiply_subtract_fusion.1.own_ref), channel_id=1, source_target_pairs={{1,0},{2,1},{3,2},{4,3},{5,4},{6,5},{7,6},{8,7},{9,8},{10,9},{11,1... | collective-permute-start | bytes 1572872 | tf_op jit(solution)/shard_map/ppermute | solution.py:26
  88.3 7.7 %collective-permute-done.6.below_ref = f32[2,256,256]{2,1,0:T(8,128)S(1)} collective-permute-done((f32[2,256,256]{2,1,0:T(8,128)S(1)}, f32[2,256,256]{2,1,0:T(8,128)S(1)}, u32[]{:S(2)}, u32[]{:S(2)}) %collective-permute-start.6) | collective-permute-done | bytes 524320 | tf_op jit(solution)/shard_map/ppermute | solution.py:26
  99.1 9.1 %collective-permute-done.8.diag_ref = f32[2,256,256]{2,1,0:T(8,128)S(1)} collective-permute-done((f32[2,256,256]{2,1,0:T(8,128)S(1)}, f32[2,256,256]{2,1,0:T(8,128)S(1)}, u32[]{:S(2)}, u32[]{:S(2)}) %collective-permute-start.8) | collective-permute-done | bytes 524320 | tf_op jit(solution)/shard_map/ppermute | solution.py:26
  108.2 19.1 %shard_map.84 = (f32[2,256,256]{2,1,0:T(8,128)S(1)}, f32[2,256,256]{2,1,0:T(8,128)S(1)}, f32[2,256,256]{2,1,0:T(8,128)S(1)}, f32[2,256,256]{2,1,0:T(8,128)S(1)}) custom-call(s32[6,2]{1,0:T(8,128)S(1)} %copy.9.offsets_ref, s32[1]{0:T(128)} %bitcast.4.count_ref, f32[2,256,256]{2,1,0:T(8,128)S(1)} %multiply_subtract_fusion.1.own_ref, ...), custom_call_target="tpu_custom_call" | custom-call | tf_op jit(solution)/shard_map/pallas_call | solution.py:191
  127.3 1.9 %collective-permute-start.10 = (f32[2,256,256]{2,1,0:T(8,128)S(1)}, f32[2,256,256]{2,1,0:T(8,128)S(1)}, u32[]{:S(2)}, u32[]{:S(2)}) collective-permute-start(f32[2,256,256]{2,1,0:T(8,128)S(1)} %get-tuple-element.20), channel_id=1, source_target_pairs={{0,1},{1,2},{2,3},{3,4},{4,5},{5,6},{6,7},{7,8},{8,9},{9,10},{10,1... | collective-permute-start | bytes 1572872 | tf_op jit(solution)/shard_map/ppermute | solution.py:26
  129.2 1.9 %collective-permute-start.9 = (f32[2,256,256]{2,1,0:T(8,128)S(1)}, f32[2,256,256]{2,1,0:T(8,128)S(1)}, u32[]{:S(2)}, u32[]{:S(2)}) collective-permute-start(f32[2,256,256]{2,1,0:T(8,128)S(1)} %get-tuple-element.18), channel_id=1, source_target_pairs={{0,1},{1,2},{2,3},{3,4},{4,5},{5,6},{6,7},{7,8},{8,9},{9,10},{10,1... | collective-permute-start | bytes 1572872 | tf_op jit(solution)/shard_map/ppermute | solution.py:26
  131.1 4.2 %collective-permute-done.10 = f32[2,256,256]{2,1,0:T(8,128)S(1)} collective-permute-done((f32[2,256,256]{2,1,0:T(8,128)S(1)}, f32[2,256,256]{2,1,0:T(8,128)S(1)}, u32[]{:S(2)}, u32[]{:S(2)}) %collective-permute-start.10) | collective-permute-done | bytes 524320 | tf_op jit(solution)/shard_map/ppermute | solution.py:26
  135.4 1.9 %collective-permute-start.11 = (f32[2,256,256]{2,1,0:T(8,128)S(1)}, f32[2,256,256]{2,1,0:T(8,128)S(1)}, u32[]{:S(2)}, u32[]{:S(2)}) collective-permute-start(f32[2,256,256]{2,1,0:T(8,128)S(1)} %add.22), channel_id=1, source_target_pairs={{0,16},{16,32},{32,48},{48,64},{64,80},{80,96},{96,112},{1,17},{17... | collective-permute-start | bytes 1572872 | tf_op jit(solution)/shard_map/ppermute | solution.py:26
  137.3 3.6 %collective-permute-done.9 = f32[2,256,256]{2,1,0:T(8,128)S(1)} collective-permute-done((f32[2,256,256]{2,1,0:T(8,128)S(1)}, f32[2,256,256]{2,1,0:T(8,128)S(1)}, u32[]{:S(2)}, u32[]{:S(2)}) %collective-permute-start.9) | collective-permute-done | bytes 524320 | tf_op jit(solution)/shard_map/ppermute | solution.py:26
  140.9 13.5 %collective-permute-done.11 = f32[2,256,256]{2,1,0:T(8,128)S(1)} collective-permute-done((f32[2,256,256]{2,1,0:T(8,128)S(1)}, f32[2,256,256]{2,1,0:T(8,128)S(1)}, u32[]{:S(2)}, u32[]{:S(2)}) %collective-permute-start.11) | collective-permute-done | bytes 524320 | tf_op jit(solution)/shard_map/ppermute | solution.py:26
  (12 shorter events, 5.1 us)
Async XLA Ops:
  0.0 15.4 %collective-permute-start = (f32[2,256,256]{2,1,0:T(8,128)}, f32[2,256,256]{2,1,0:T(8,128)S(1)}, u32[]{:S(2)}, u32[]{:S(2)}) collective-permute-start(f32[2,256,256]{2,1,0:T(8,128)} %own_ref.1), channel_id=1, source_target_pairs={{16,0},{32,16},{48,32},{64,48},{80,64},{96,80},{112,96},{17,1},{33... | collective-permute-start | bytes 1572872 | tf_op jit(solution)/shard_map/ppermute | solution.py:26
  4.5 24.2 %collective-permute-start.1 = (f32[2,256,256]{2,1,0:T(8,128)}, f32[2,256,256]{2,1,0:T(8,128)S(1)}, u32[]{:S(2)}, u32[]{:S(2)}) collective-permute-start(f32[2,256,256]{2,1,0:T(8,128)} %own_ref.1), channel_id=1, source_target_pairs={{1,0},{2,1},{3,2},{4,3},{5,4},{6,5},{7,6},{8,7},{9,8},{10,9},{11,1... | collective-permute-start | bytes 1572872 | tf_op jit(solution)/shard_map/ppermute | solution.py:26
  15.4 16.7 %collective-permute-start.2 = (f32[2,256,256]{2,1,0:T(8,128)S(1)}, f32[2,256,256]{2,1,0:T(8,128)S(1)}, u32[]{:S(2)}, u32[]{:S(2)}) collective-permute-start(f32[2,256,256]{2,1,0:T(8,128)S(1)} %collective-permute-done.below_ref), channel_id=1, source_target_pairs={{1,0},{2,1},{3,2},{4,3},{5,4},{6,5},{7,6},{8,7},{9,8},{10,9},{11,1... | collective-permute-start | bytes 1572872 | tf_op jit(solution)/shard_map/ppermute | solution.py:26
  20.2 11.8 %copy-start = (f32[2,256,256]{2,1,0:T(8,128)S(1)}, f32[2,256,256]{2,1,0:T(8,128)}, u32[]{:S(2)}) copy-start(f32[2,256,256]{2,1,0:T(8,128)} %own_ref.1) | copy-start | bytes 1572868
  20.2 11.8 %copy-start.1 = (bf16[4,256,256]{2,1,0:T(8,128)(2,1)S(1)}, bf16[4,256,256]{2,1,0:T(8,128)(2,1)}, u32[]{:S(2)}) copy-start(bf16[4,256,256]{2,1,0:T(8,128)(2,1)} %constant.10.clone.table_ref) | copy-start | bytes 1572868
  51.0 8.0 %collective-permute-start.4 = (f32[2,256,256]{2,1,0:T(8,128)S(1)}, f32[2,256,256]{2,1,0:T(8,128)S(1)}, u32[]{:S(2)}, u32[]{:S(2)}) collective-permute-start(f32[2,256,256]{2,1,0:T(8,128)S(1)} %get-tuple-element.16), channel_id=1, source_target_pairs={{0,1},{1,2},{2,3},{3,4},{4,5},{5,6},{6,7},{7,8},{8,9},{9,10},{10,1... | collective-permute-start | bytes 1572872 | tf_op jit(solution)/shard_map/ppermute | solution.py:26
  53.0 11.7 %collective-permute-start.3 = (f32[2,256,256]{2,1,0:T(8,128)S(1)}, f32[2,256,256]{2,1,0:T(8,128)S(1)}, u32[]{:S(2)}, u32[]{:S(2)}) collective-permute-start(f32[2,256,256]{2,1,0:T(8,128)S(1)} %get-tuple-element.14), channel_id=1, source_target_pairs={{0,1},{1,2},{2,3},{3,4},{4,5},{5,6},{6,7},{7,8},{8,9},{9,10},{10,1... | collective-permute-start | bytes 1572872 | tf_op jit(solution)/shard_map/ppermute | solution.py:26
  59.1 23.5 %collective-permute-start.5 = (f32[2,256,256]{2,1,0:T(8,128)S(1)}, f32[2,256,256]{2,1,0:T(8,128)S(1)}, u32[]{:S(2)}, u32[]{:S(2)}) collective-permute-start(f32[2,256,256]{2,1,0:T(8,128)S(1)} %add.19), channel_id=1, source_target_pairs={{0,16},{16,32},{32,48},{48,64},{64,80},{80,96},{96,112},{1,17},{17... | collective-permute-start | bytes 1572872 | tf_op jit(solution)/shard_map/ppermute | solution.py:26
  82.7 13.2 %collective-permute-start.6 = (f32[2,256,256]{2,1,0:T(8,128)S(1)}, f32[2,256,256]{2,1,0:T(8,128)S(1)}, u32[]{:S(2)}, u32[]{:S(2)}) collective-permute-start(f32[2,256,256]{2,1,0:T(8,128)S(1)} %multiply_subtract_fusion.1.own_ref), channel_id=1, source_target_pairs={{16,0},{32,16},{48,32},{64,48},{80,64},{96,80},{112,96},{17,1},{33... | collective-permute-start | bytes 1572872 | tf_op jit(solution)/shard_map/ppermute | solution.py:26
  86.4 12.7 %collective-permute-start.7 = (f32[2,256,256]{2,1,0:T(8,128)S(1)}, f32[2,256,256]{2,1,0:T(8,128)S(1)}, u32[]{:S(2)}, u32[]{:S(2)}) collective-permute-start(f32[2,256,256]{2,1,0:T(8,128)S(1)} %multiply_subtract_fusion.1.own_ref), channel_id=1, source_target_pairs={{1,0},{2,1},{3,2},{4,3},{5,4},{6,5},{7,6},{8,7},{9,8},{10,9},{11,1... | collective-permute-start | bytes 1572872 | tf_op jit(solution)/shard_map/ppermute | solution.py:26
  96.0 12.2 %collective-permute-start.8 = (f32[2,256,256]{2,1,0:T(8,128)S(1)}, f32[2,256,256]{2,1,0:T(8,128)S(1)}, u32[]{:S(2)}, u32[]{:S(2)}) collective-permute-start(f32[2,256,256]{2,1,0:T(8,128)S(1)} %collective-permute-done.6.below_ref), channel_id=1, source_target_pairs={{1,0},{2,1},{3,2},{4,3},{5,4},{6,5},{7,6},{8,7},{9,8},{10,9},{11,1... | collective-permute-start | bytes 1572872 | tf_op jit(solution)/shard_map/ppermute | solution.py:26
  127.3 8.0 %collective-permute-start.10 = (f32[2,256,256]{2,1,0:T(8,128)S(1)}, f32[2,256,256]{2,1,0:T(8,128)S(1)}, u32[]{:S(2)}, u32[]{:S(2)}) collective-permute-start(f32[2,256,256]{2,1,0:T(8,128)S(1)} %get-tuple-element.20), channel_id=1, source_target_pairs={{0,1},{1,2},{2,3},{3,4},{4,5},{5,6},{6,7},{7,8},{8,9},{9,10},{10,1... | collective-permute-start | bytes 1572872 | tf_op jit(solution)/shard_map/ppermute | solution.py:26
  129.2 11.7 %collective-permute-start.9 = (f32[2,256,256]{2,1,0:T(8,128)S(1)}, f32[2,256,256]{2,1,0:T(8,128)S(1)}, u32[]{:S(2)}, u32[]{:S(2)}) collective-permute-start(f32[2,256,256]{2,1,0:T(8,128)S(1)} %get-tuple-element.18), channel_id=1, source_target_pairs={{0,1},{1,2},{2,3},{3,4},{4,5},{5,6},{6,7},{7,8},{8,9},{9,10},{10,1... | collective-permute-start | bytes 1572872 | tf_op jit(solution)/shard_map/ppermute | solution.py:26
  135.4 19.0 %collective-permute-start.11 = (f32[2,256,256]{2,1,0:T(8,128)S(1)}, f32[2,256,256]{2,1,0:T(8,128)S(1)}, u32[]{:S(2)}, u32[]{:S(2)}) collective-permute-start(f32[2,256,256]{2,1,0:T(8,128)S(1)} %add.22), channel_id=1, source_target_pairs={{0,16},{16,32},{32,48},{48,64},{64,80},{80,96},{96,112},{1,17},{17... | collective-permute-start | bytes 1572872 | tf_op jit(solution)/shard_map/ppermute | solution.py:26

commit v2 on v1

v2 whole, which is shorter than its diff:
```python
import functools
import math

import jax
import jax.numpy as jnp
import ml_dtypes
import numpy as np
from jax import lax
from jax.experimental import pallas as pl
from jax.experimental.pallas import tpu as pltpu
from jax.sharding import PartitionSpec as P

ITERS = 2
STEP = 0.1
DAMPING = 0.1
SIDE = 256
HALF = 128
SUB = 8
CHUNK = 16
H_SPLIT = [[False, False, True, True], [True, False, True, True]]
G_SPLIT = [[True, False, True, True], [True, False, True, True]]
AHEAD = 1
F32 = jnp.float32
BF16 = jnp.bfloat16
VMEM = pl.BlockSpec(memory_space=pltpu.VMEM)
SMEM = pl.BlockSpec(memory_space=pltpu.SMEM)


def from_behind(block, axis, distance):
    devices = range(lax.axis_size(axis))
    route = [(i - distance, i) for i in devices if i - distance in devices]
    return lax.ppermute(block, axis, route)


def tables():
    ladder = np.arange(SIDE, dtype=np.int32)
    theta = (ladder[:, None] * ladder[None, :] % SIDE).astype(np.float32)
    theta = theta * np.float32(2.0 * math.pi / SIDE)
    factor = np.float32(1.0 / math.sqrt(SIDE))
    cosine, sine = np.cos(theta) * factor, np.sin(theta) * factor
    forms = []
    for parity in (0, 1):
        c, s = cosine[parity::2, :HALF], sine[parity::2, :HALF]
        forms.append(np.block([[c, s], [-s, c]]))
    forms += [f.T for f in forms]
    return np.stack(forms).astype(ml_dtypes.bfloat16)


def parity_order():
    order = np.concatenate([np.arange(0, SIDE, 2), np.arange(1, SIDE, 2)])
    matrix = np.zeros((SIDE, SIDE), np.float32)
    matrix[order, np.arange(SIDE)] = 1.0
    return matrix.astype(ml_dtypes.bfloat16)


def sort_kernel(order_ref, amp_ref, out_ref, wide):
    def one(slot, _):
        rest, terms = amp_ref[slot], []
        for _ in range(3):
            terms.append(rest.astype(BF16))
            rest = rest - terms[-1].astype(F32)
        moved = [dot(term, order_ref[...]) for term in terms]
        whole = (moved[0] + moved[1]) + moved[2]
        for q in (0, 1):
            at = slice(q * HALF, (q + 1) * HALF)
            wide[q] = whole[:, at]
            for parity in (0, 1):
                rows_at = pl.ds(parity * HALF, HALF)
                out_ref[slot, rows_at, at] = wide[q, pl.ds(parity, HALF, stride=2), :]
        return 0

    lax.fori_loop(0, amp_ref.shape[0], one, 0)


def sort_amplitude(amplitude):
    return pl.pallas_call(
        sort_kernel,
        out_shape=jax.ShapeDtypeStruct(amplitude.shape, F32),
        in_specs=[VMEM, VMEM],
        out_specs=VMEM,
        scratch_shapes=[pltpu.VMEM((2, SIDE, HALF), F32)],
        compiler_params=pltpu.CompilerParams(vmem_limit_bytes=16 * 2**20),
        cost_estimate=pl.CostEstimate(
            flops=6 * amplitude.size * SIDE, bytes_accessed=8 * amplitude.size, transcendentals=0
        ),
    )(parity_order(), amplitude)


def dot(a, b):
    return jnp.dot(a, b, preferred_element_type=F32)


def lanes(a, b):
    return jnp.concatenate([a, b], axis=1)


def rows(a, b):
    return jnp.concatenate([a, b], axis=0)


def in_turn(modes, first, second):
    held = []
    for m in range(modes + AHEAD):
        if m < modes:
            held.append(first(m))
        if m >= AHEAD:
            second(m - AHEAD, held[m - AHEAD])


def places(splits):
    found = []
    for index, split in enumerate(splits):
        at = pl.ds(index // 2 * SIDE, SIDE)
        for part in (0, 1) if split else (slice(None),):
            found.append((index % 2, part, at))
    return found


def update_kernel(in_splits, out_splits, offsets_ref, count_ref, *refs):
    tile_at, out_at = places(in_splits), places(out_splits)
    tiles, refs = refs[: len(tile_at)], refs[len(tile_at) :]
    (probe_ref, amp_ref, table_ref), refs = refs[:3], refs[3:]
    outs, scratch = refs[: len(out_at)], refs[len(out_at) :]
    left_ext, right_ext, left_sum, right_sum, patch, far, chis, grad = scratch
    modes = probe_ref.shape[0]
    for tile, (half, part, at) in zip(tiles, tile_at):
        (left_ext, right_ext)[half][part, at] = tile[...]
    left_sum[...] = jnp.zeros_like(left_sum)
    right_sum[...] = jnp.zeros_like(right_sum)
    groups = SIDE // SUB
    column = lax.broadcasted_iota(jnp.int32, (SIDE + SUB, SIDE), 1)
    lane = lax.broadcasted_iota(jnp.int32, (groups, SUB, SIDE), 1)

    def position(slot, _):
        top, left = offsets_ref[0, 0, slot, 0], offsets_ref[0, 0, slot, 1]
        shift = lax.rem(top, SUB)
        window = pl.ds(pl.multiple_of(top - shift, SUB), SIDE + SUB)
        beside = column >= left
        for part in (0, 1):
            mixed = jnp.where(beside, left_ext[part, window, :], right_ext[part, window, :])
            mixed = pltpu.roll(mixed, lax.rem(SIDE - left, SIDE), 1)
            mixed = mixed.reshape(groups + 1, SUB, SIDE)
            mixed = pltpu.roll(mixed, lax.rem(SUB - shift, SUB), 1)
            mixed = jnp.where(lane < SUB - shift, mixed[:-1], mixed[1:])
            patch[part] = mixed.reshape(SIDE, SIDE)
        def section(m):
            psi = []
            for half in (0, 1):
                at = pl.ds(half * HALF, HALF)
                pr, pi = probe_ref[m, 0, at, :], probe_ref[m, 1, at, :]
                xr, xi = patch[0, at, :], patch[1, at, :]
                psi.append(rows(pr * xr - pi * xi, pr * xi + pi * xr))
            even = dot(table_ref[0], (psi[0] + psi[1]).astype(BF16))
            odd = dot(table_ref[1], (psi[0] - psi[1]).astype(BF16))
            sums, differences = [], []
            for s in (even, odd):
                a, b = s[:, :HALF], s[:, HALF:]
                u, v = (a + b).astype(BF16), (a - b).astype(BF16)
                sums.append(lanes(u[:HALF], u[HALF:]))
                differences.append(lanes(v[:HALF], v[HALF:]))
            return rows(*sums), rows(*differences)

        def spread(m, blocks):
            for q, block in enumerate(blocks):
                far[m, q] = dot(block, table_ref[2 + q])

        def back(m):
            halves = []
            for parity in (0, 1):
                at = pl.ds(parity * HALF, HALF)
                c = [chis[m, q, at, :] for q in (0, 1)]
                real = lanes(c[0][:, :HALF], c[1][:, :HALF])
                imag = lanes(c[0][:, HALF:], c[1][:, HALF:])
                halves.append(dot(table_ref[2 + parity], rows(real, imag)))
            top_back = (halves[0] + halves[1]).astype(BF16)
            bottom_back = (halves[0] - halves[1]).astype(BF16)
            blocks = []
            for q in (0, 1):
                at = slice(q * HALF, (q + 1) * HALF)
                blocks.append(
                    rows(
                        lanes(top_back[:HALF, at], top_back[HALF:, at]),
                        lanes(bottom_back[:HALF, at], bottom_back[HALF:, at]),
                    )
                )
            return blocks

        def gather(m, blocks):
            wave = [dot(block, table_ref[q]) for q, block in enumerate(blocks)]
            for side, w in ((0, wave[0] + wave[1]), (1, wave[0] - wave[1])):
                at = pl.ds(side * HALF, HALF)
                pr, pi = probe_ref[m, 0, :, at], probe_ref[m, 1, :, at]
                wr, wi = w[:, :HALF], w[:, HALF:]
                gr, gi = pr * wr + pi * wi, pr * wi - pi * wr
                if m:
                    gr, gi = gr + grad[0, :, at], gi + grad[1, :, at]
                grad[0, :, at] = gr
                grad[1, :, at] = gi

        in_turn(modes, section, spread)
        for q in (0, 1):
            for start in range(0, SIDE, CHUNK):
                at = pl.ds(start, CHUNK)
                f = [far[m, q, at, :] for m in range(modes)]
                squares = [x * x for x in f]
                power = sum(squares[1:], squares[0])
                power = power[:, :HALF] + power[:, HALF:]
                measured = amp_ref[slot, at, q * HALF : (q + 1) * HALF]
                ratio = 1.0 - measured * lax.rsqrt(power + DAMPING)
                ratio = lanes(ratio, ratio)
                for m in range(modes):
                    chis[m, q, at, :] = (f[m] * ratio).astype(BF16)
        in_turn(modes, back, gather)
        empty = jnp.zeros((1, SUB, SIDE), F32)
        for part in (0, 1):
            turned = pltpu.roll(grad[part], left, 1).reshape(groups, SUB, SIDE)
            turned = pltpu.roll(turned, shift, 1)
            first = jnp.concatenate([jnp.where(lane < shift, 0.0, turned), empty], axis=0)
            second = jnp.concatenate([empty, jnp.where(lane < shift, turned, 0.0)], axis=0)
            turned = (first + second).reshape(SIDE + SUB, SIDE)
            left_sum[part, window, :] += jnp.where(beside, turned, 0.0)
            right_sum[part, window, :] += jnp.where(beside, 0.0, turned)
        return 0

    lax.fori_loop(0, count_ref[0, 0], position, 0)
    for out, (half, part, at) in zip(outs, out_at):
        out[...] = (left_sum, right_sum)[half][part, at]


def gradient(offsets, count, own, right, below, diag, probe, amplitude, table, out_splits):
    modes = probe.shape[0]
    tall = pltpu.VMEM((2, 2 * SIDE, SIDE), F32)
    tile, plane = (2, SIDE, SIDE), (SIDE, SIDE)
    given = [own, right, below, diag]
    in_splits = [len(x) > 1 for x in given]
    shapes = [jax.ShapeDtypeStruct(s, F32) for x in out_splits for s in ([plane] * 2 if x else [tile])]
    sums = iter(
        pl.pallas_call(
            functools.partial(update_kernel, in_splits, out_splits),
            out_shape=shapes,
            in_specs=[SMEM, SMEM] + [VMEM] * (sum(map(len, given)) + 3),
            out_specs=[VMEM] * len(shapes),
            scratch_shapes=[
                tall,
                tall,
                tall,
                tall,
                pltpu.VMEM(tile, F32),
                pltpu.VMEM((modes, 2, SIDE, SIDE), F32),
                pltpu.VMEM((modes, 2, SIDE, SIDE), BF16),
                pltpu.VMEM(tile, F32),
            ],
            compiler_params=pltpu.CompilerParams(vmem_limit_bytes=24 * 2**20),
        )(offsets, count, *own, *right, *below, *diag, probe, amplitude, table)
    )
    return [[next(sums) for _ in range(2 if x else 1)] for x in out_splits]


def body(object_field, probe_modes, positions, counts, amplitude):
    table = tables()
    sorted_amp = sort_amplitude(amplitude[0, 0])
    def planes(arrays):
        return arrays if len(arrays) > 1 else [arrays[0][part] for part in (0, 1)]

    def shaped(arrays, split):
        if split:
            return planes(arrays)
        return arrays if len(arrays) == 1 else [jnp.stack(arrays)]

    field = [object_field]
    for sweep in range(ITERS):
        h_split = H_SPLIT[sweep]
        g_split = G_SPLIT[sweep]
        right = [from_behind(f, "col", -1) for f in shaped(field, h_split[1])]
        below = [from_behind(f, "row", -1) for f in shaped(field, h_split[2])]
        diag = [from_behind(b, "col", -1) for b in below]
        own_sum, right_sum, below_sum, diag_sum = gradient(
            positions, counts, field, right, below, diag, probe_modes, sorted_amp, table, g_split
        )
        diag_sum = [from_behind(d, "col", 1) for d in diag_sum]
        from_above = [from_behind(b + d, "row", 1) for b, d in zip(below_sum, diag_sum)]
        from_left = [from_behind(r, "col", 1) for r in right_sum]
        if g_split[2]:
            field = [
                lax.optimization_barrier(f - STEP * (o + l + a))
                for f, o, l, a in zip(planes(field), planes(own_sum), planes(from_left), from_above)
            ]
        else:
            field = [field[0] - STEP * (own_sum[0] + from_left[0] + from_above[0])]
    return shaped(field, False)[0]


def solution(mesh):
    placed = (
        P(None, "row", "col"),
        P(),
        P("row", "col", None, None),
        P("row", "col"),
        P("row", "col", None, None, None),
    )
    return jax.shard_map(
        body, mesh=mesh, in_specs=placed, out_specs=P(None, "row", "col"), check_vma=False
    )
```

time: 155 us -> 134 us (0.86)
  the two profiles are of different devices: /device:TPU:101 before, /device:TPU:38 now
where the time goes in v2:
time: 134 us; the launch traced here: 133 us
  starting transfers between devices  54.8 us (41%)
  waiting for transfers between devices  39.8 us (30%)
  Pallas kernels  32.5 us (24%)
  local copies, waits for them, and re-layouts  4.15 us (3%)
    ppermute x20, starting transfers between devices, from_behind(): return lax.ppermute(block, axis, route)  54.8 us
    ppermute x20, waiting for transfers between devices, from_behind(): return lax.ppermute(block, axis, route)  39.8 us
    pallas_call x2, Pallas kernels, gradient(): pl.pallas_call(functools.partial(update_kernel, in_splits, out_splits), o...  30.7 us
    unnamed x11, local copies, waits for them, and re-layouts  3.09 us
  transfers between devices with their start and end apart: 20, of which 11 were waited for; matrix products, arithmetic and copies ran while one was open for 1% of the time, Pallas kernels for 1%

profile of v2, /device:TPU:38, one launch (start us, length us, event | category | flops | bytes accessed | tf_op | source)
XLA Modules:
  0.0 133.5 jit_solution(1430800480375716487)
XLA Ops:
  1.1 4.5 %collective-permute-start.2 = (f32[256,256]{1,0:T(8,128)S(1)}, f32[256,256]{1,0:T(8,128)S(1)}, u32[]{:S(2)}, u32[]{:S(2)}) collective-permute-start(f32[256,256]{1,0:T(8,128)S(1)} %get-tuple-element.37), channel_id=1, source_target_pairs={{16,0},{32,16},{48,32},{64,48},{80,64},{96,80},{112,96},{17,1},{33... | collective-permute-start | bytes 786440 | tf_op jit(solution)/shard_map/ppermute | solution.py:32
  5.5 2.7 %collective-permute-start.1 = (f32[256,256]{1,0:T(8,128)S(1)}, f32[256,256]{1,0:T(8,128)S(1)}, u32[]{:S(2)}, u32[]{:S(2)}) collective-permute-start(f32[256,256]{1,0:T(8,128)S(1)} %get-tuple-element.38), channel_id=1, source_target_pairs={{16,0},{32,16},{48,32},{64,48},{80,64},{96,80},{112,96},{17,1},{33... | collective-permute-start | bytes 786440 | tf_op jit(solution)/shard_map/ppermute | solution.py:32
  8.2 1.9 %collective-permute-start = (f32[2,256,256]{2,1,0:T(8,128)}, f32[2,256,256]{2,1,0:T(8,128)S(1)}, u32[]{:S(2)}, u32[]{:S(2)}) collective-permute-start(f32[2,256,256]{2,1,0:T(8,128)} %refs_0_.1), channel_id=1, source_target_pairs={{1,0},{2,1},{3,2},{4,3},{5,4},{6,5},{7,6},{8,7},{9,8},{10,9},{11,1... | collective-permute-start | bytes 1572872 | tf_op jit(solution)/shard_map/ppermute | solution.py:32
  10.1 2.1 %collective-permute-done.2.refs_3_ = f32[256,256]{1,0:T(8,128)S(1)} collective-permute-done((f32[256,256]{1,0:T(8,128)S(1)}, f32[256,256]{1,0:T(8,128)S(1)}, u32[]{:S(2)}, u32[]{:S(2)}) %collective-permute-start.2) | collective-permute-done | bytes 262176 | tf_op jit(solution)/shard_map/ppermute | solution.py:32
  14.1 2.6 %collective-permute-done.1.refs_2_ = f32[256,256]{1,0:T(8,128)S(1)} collective-permute-done((f32[256,256]{1,0:T(8,128)S(1)}, f32[256,256]{1,0:T(8,128)S(1)}, u32[]{:S(2)}, u32[]{:S(2)}) %collective-permute-start.1) | collective-permute-done | bytes 262176 | tf_op jit(solution)/shard_map/ppermute | solution.py:32
  24.2 15.4 %shard_map.74 = (f32[256,256]{1,0:T(8,128)S(1)}, f32[256,256]{1,0:T(8,128)S(1)}, f32[2,256,256]{2,1,0:T(8,128)S(1)}, f32[256,256]{1,0:T(8,128)S(1)}, f32[256,256...) custom-call(s32[1,1,6,2]{3,2,1,0:T(8,128)S(1)} %copy.8.offsets_ref, s32[1,1]{1,0:T(1,128)S(6)} %copy.10.count_ref, ...), custom_call_target="tpu_custom_call" | custom-call | tf_op jit(solution)/shard_map/pallas_call | solution.py:238
  39.6 5.1 %collective-permute-start.6 = (f32[256,256]{1,0:T(8,128)S(1)}, f32[256,256]{1,0:T(8,128)S(1)}, u32[]{:S(2)}, u32[]{:S(2)}) collective-permute-start(f32[256,256]{1,0:T(8,128)S(1)} %get-tuple-element.22), channel_id=1, source_target_pairs={{0,1},{1,2},{2,3},{3,4},{4,5},{5,6},{6,7},{7,8},{8,9},{9,10},{10,1... | collective-permute-start | bytes 786440 | tf_op jit(solution)/shard_map/ppermute | solution.py:32
  44.7 1.9 %collective-permute-start.8 = (f32[256,256]{1,0:T(8,128)S(1)}, f32[256,256]{1,0:T(8,128)S(1)}, u32[]{:S(2)}, u32[]{:S(2)}) collective-permute-start(f32[256,256]{1,0:T(8,128)S(1)} %get-tuple-element.25), channel_id=1, source_target_pairs={{0,1},{1,2},{2,3},{3,4},{4,5},{5,6},{6,7},{7,8},{8,9},{9,10},{10,1... | collective-permute-start | bytes 786440 | tf_op jit(solution)/shard_map/ppermute | solution.py:32
  46.7 1.9 %collective-permute-start.5 = (f32[2,256,256]{2,1,0:T(8,128)S(1)}, f32[2,256,256]{2,1,0:T(8,128)S(1)}, u32[]{:S(2)}, u32[]{:S(2)}) collective-permute-start(f32[2,256,256]{2,1,0:T(8,128)S(1)} %get-tuple-element.20), channel_id=1, source_target_pairs={{0,1},{1,2},{2,3},{3,4},{4,5},{5,6},{6,7},{7,8},{8,9},{9,10},{10,1... | collective-permute-start | bytes 1572872 | tf_op jit(solution)/shard_map/ppermute | solution.py:32
  48.6 3.2 %collective-permute-start.7 = (f32[256,256]{1,0:T(8,128)S(1)}, f32[256,256]{1,0:T(8,128)S(1)}, u32[]{:S(2)}, u32[]{:S(2)}) collective-permute-start(f32[256,256]{1,0:T(8,128)S(1)} %add.37), channel_id=1, source_target_pairs={{0,16},{16,32},{32,48},{48,64},{64,80},{80,96},{96,112},{1,17},{17... | collective-permute-start | bytes 786440 | tf_op jit(solution)/shard_map/ppermute | solution.py:32
  52.5 3.2 %collective-permute-start.9 = (f32[256,256]{1,0:T(8,128)S(1)}, f32[256,256]{1,0:T(8,128)S(1)}, u32[]{:S(2)}, u32[]{:S(2)}) collective-permute-start(f32[256,256]{1,0:T(8,128)S(1)} %add.40), channel_id=1, source_target_pairs={{0,16},{16,32},{32,48},{48,64},{64,80},{80,96},{96,112},{1,17},{17... | collective-permute-start | bytes 786440 | tf_op jit(solution)/shard_map/ppermute | solution.py:32
  55.6 6.1 %collective-permute-done.7 = f32[256,256]{1,0:T(8,128)S(1)} collective-permute-done((f32[256,256]{1,0:T(8,128)S(1)}, f32[256,256]{1,0:T(8,128)S(1)}, u32[]{:S(2)}, u32[]{:S(2)}) %collective-permute-start.7) | collective-permute-done | bytes 262176 | tf_op jit(solution)/shard_map/ppermute | solution.py:32
  61.8 5.0 %collective-permute-done.9 = f32[256,256]{1,0:T(8,128)S(1)} collective-permute-done((f32[256,256]{1,0:T(8,128)S(1)}, f32[256,256]{1,0:T(8,128)S(1)}, u32[]{:S(2)}, u32[]{:S(2)}) %collective-permute-start.9) | collective-permute-done | bytes 262176 | tf_op jit(solution)/shard_map/ppermute | solution.py:32
  66.9 3.6 %collective-permute-start.12 = (f32[256,256]{1,0:T(8,128)S(1)}, f32[256,256]{1,0:T(8,128)S(1)}, u32[]{:S(2)}, u32[]{:S(2)}) collective-permute-start(f32[256,256]{1,0:T(8,128)S(1)} %get-tuple-element.34.refs_1_), channel_id=1, source_target_pairs={{16,0},{32,16},{48,32},{64,48},{80,64},{96,80},{112,96},{17,1},{33... | collective-permute-start | bytes 786440 | tf_op jit(solution)/shard_map/ppermute | solution.py:32
  70.6 2.5 %collective-permute-start.10 = (f32[2,256,256]{2,1,0:T(8,128)S(1)}, f32[2,256,256]{2,1,0:T(8,128)S(1)}, u32[]{:S(2)}, u32[]{:S(2)}) collective-permute-start(f32[2,256,256]{2,1,0:T(8,128)S(1)} %pad_maximum_fusion), channel_id=1, source_target_pairs={{1,0},{2,1},{3,2},{4,3},{5,4},{6,5},{7,6},{8,7},{9,8},{10,9},{11,1... | collective-permute-start | bytes 1572872 | tf_op jit(solution)/shard_map/ppermute | solution.py:32
  73.1 2.2 %collective-permute-start.11 = (f32[256,256]{1,0:T(8,128)S(1)}, f32[256,256]{1,0:T(8,128)S(1)}, u32[]{:S(2)}, u32[]{:S(2)}) collective-permute-start(f32[256,256]{1,0:T(8,128)S(1)} %get-tuple-element.33.refs_0_), channel_id=1, source_target_pairs={{16,0},{32,16},{48,32},{64,48},{80,64},{96,80},{112,96},{17,1},{33... | collective-permute-start | bytes 786440 | tf_op jit(solution)/shard_map/ppermute | solution.py:32
  76.5 2.2 %collective-permute-start.14 = (f32[256,256]{1,0:T(8,128)S(1)}, f32[256,256]{1,0:T(8,128)S(1)}, u32[]{:S(2)}, u32[]{:S(2)}) collective-permute-start(f32[256,256]{1,0:T(8,128)S(1)} %collective-permute-done.12.refs_4_), channel_id=1, source_target_pairs={{1,0},{2,1},{3,2},{4,3},{5,4},{6,5},{7,6},{8,7},{9,8},{10,9},{11,1... | collective-permute-start | bytes 786440 | tf_op jit(solution)/shard_map/ppermute | solution.py:32
  78.7 4.4 %collective-permute-done.11.refs_3_ = f32[256,256]{1,0:T(8,128)S(1)} collective-permute-done((f32[256,256]{1,0:T(8,128)S(1)}, f32[256,256]{1,0:T(8,128)S(1)}, u32[]{:S(2)}, u32[]{:S(2)}) %collective-permute-start.11) | collective-permute-done | bytes 262176 | tf_op jit(solution)/shard_map/ppermute | solution.py:32
  83.1 3.3 %collective-permute-start.13 = (f32[256,256]{1,0:T(8,128)S(1)}, f32[256,256]{1,0:T(8,128)S(1)}, u32[]{:S(2)}, u32[]{:S(2)}) collective-permute-start(f32[256,256]{1,0:T(8,128)S(1)} %collective-permute-done.11.refs_3_), channel_id=1, source_target_pairs={{1,0},{2,1},{3,2},{4,3},{5,4},{6,5},{7,6},{8,7},{9,8},{10,9},{11,1... | collective-permute-start | bytes 786440 | tf_op jit(solution)/shard_map/ppermute | solution.py:32
  86.5 3.8 %collective-permute-done.13.refs_5_ = f32[256,256]{1,0:T(8,128)S(1)} collective-permute-done((f32[256,256]{1,0:T(8,128)S(1)}, f32[256,256]{1,0:T(8,128)S(1)}, u32[]{:S(2)}, u32[]{:S(2)}) %collective-permute-start.13) | collective-permute-done | bytes 262176 | tf_op jit(solution)/shard_map/ppermute | solution.py:32
  90.3 15.3 %shard_map.75 = (f32[256,256]{1,0:T(8,128)S(1)}, f32[256,256]{1,0:T(8,128)S(1)}, f32[2,256,256]{2,1,0:T(8,128)S(1)}, f32[256,256]{1,0:T(8,128)S(1)}, f32[256,256...) custom-call(s32[1,1,6,2]{3,2,1,0:T(8,128)S(1)} %copy.8.offsets_ref, s32[1,1]{1,0:T(1,128)S(6)} %copy.10.count_ref, ...), custom_call_target="tpu_custom_call" | custom-call | tf_op jit(solution)/shard_map/pallas_call | solution.py:238
  105.7 5.0 %collective-permute-start.16 = (f32[256,256]{1,0:T(8,128)S(1)}, f32[256,256]{1,0:T(8,128)S(1)}, u32[]{:S(2)}, u32[]{:S(2)}) collective-permute-start(f32[256,256]{1,0:T(8,128)S(1)} %get-tuple-element.29), channel_id=1, source_target_pairs={{0,1},{1,2},{2,3},{3,4},{4,5},{5,6},{6,7},{7,8},{8,9},{9,10},{10,1... | collective-permute-start | bytes 786440 | tf_op jit(solution)/shard_map/ppermute | solution.py:32
  120.4 7.4 %collective-permute-done.17 = f32[256,256]{1,0:T(8,128)S(1)} collective-permute-done((f32[256,256]{1,0:T(8,128)S(1)}, f32[256,256]{1,0:T(8,128)S(1)}, u32[]{:S(2)}, u32[]{:S(2)}) %collective-permute-start.17) | collective-permute-done | bytes 262176 | tf_op jit(solution)/shard_map/ppermute | solution.py:32
  127.8 4.7 %collective-permute-done.19 = f32[256,256]{1,0:T(8,128)S(1)} collective-permute-done((f32[256,256]{1,0:T(8,128)S(1)}, f32[256,256]{1,0:T(8,128)S(1)}, u32[]{:S(2)}, u32[]{:S(2)}) %collective-permute-start.19) | collective-permute-done | bytes 262176 | tf_op jit(solution)/shard_map/ppermute | solution.py:32
  (39 shorter events, 22.4 us)
Async XLA Ops:
  1.1 11.2 %collective-permute-start.2 = (f32[256,256]{1,0:T(8,128)S(1)}, f32[256,256]{1,0:T(8,128)S(1)}, u32[]{:S(2)}, u32[]{:S(2)}) collective-permute-start(f32[256,256]{1,0:T(8,128)S(1)} %get-tuple-element.37), channel_id=1, source_target_pairs={{16,0},{32,16},{48,32},{64,48},{80,64},{96,80},{112,96},{17,1},{33... | collective-permute-start | bytes 786440 | tf_op jit(solution)/shard_map/ppermute | solution.py:32
  5.5 11.2 %collective-permute-start.1 = (f32[256,256]{1,0:T(8,128)S(1)}, f32[256,256]{1,0:T(8,128)S(1)}, u32[]{:S(2)}, u32[]{:S(2)}) collective-permute-start(f32[256,256]{1,0:T(8,128)S(1)} %get-tuple-element.38), channel_id=1, source_target_pairs={{16,0},{32,16},{48,32},{64,48},{80,64},{96,80},{112,96},{17,1},{33... | collective-permute-start | bytes 786440 | tf_op jit(solution)/shard_map/ppermute | solution.py:32
  8.2 16.0 %collective-permute-start = (f32[2,256,256]{2,1,0:T(8,128)}, f32[2,256,256]{2,1,0:T(8,128)S(1)}, u32[]{:S(2)}, u32[]{:S(2)}) collective-permute-start(f32[2,256,256]{2,1,0:T(8,128)} %refs_0_.1), channel_id=1, source_target_pairs={{1,0},{2,1},{3,2},{4,3},{5,4},{6,5},{7,6},{8,7},{9,8},{10,9},{11,1... | collective-permute-start | bytes 1572872 | tf_op jit(solution)/shard_map/ppermute | solution.py:32
  12.2 11.9 %collective-permute-start.4 = (f32[256,256]{1,0:T(8,128)S(1)}, f32[256,256]{1,0:T(8,128)S(1)}, u32[]{:S(2)}, u32[]{:S(2)}) collective-permute-start(f32[256,256]{1,0:T(8,128)S(1)} %collective-permute-done.2.refs_3_), channel_id=1, source_target_pairs={{1,0},{2,1},{3,2},{4,3},{5,4},{6,5},{7,6},{8,7},{9,8},{10,9},{11,1... | collective-permute-start | bytes 786440 | tf_op jit(solution)/shard_map/ppermute | solution.py:32
  16.7 7.5 %collective-permute-start.3 = (f32[256,256]{1,0:T(8,128)S(1)}, f32[256,256]{1,0:T(8,128)S(1)}, u32[]{:S(2)}, u32[]{:S(2)}) collective-permute-start(f32[256,256]{1,0:T(8,128)S(1)} %collective-permute-done.1.refs_2_), channel_id=1, source_target_pairs={{1,0},{2,1},{3,2},{4,3},{5,4},{6,5},{7,6},{8,7},{9,8},{10,9},{11,1... | collective-permute-start | bytes 786440 | tf_op jit(solution)/shard_map/ppermute | solution.py:32
  20.0 1.4 %copy-start.3 = (f32[1,1,6,256,256]{4,3,2,1,0:T(8,128)S(1)}, f32[1,1,6,256,256]{4,3,2,1,0:T(8,128)}, u32[]{:S(2)}) copy-start(f32[1,1,6,256,256]{4,3,2,1,0:T(8,128)} %param.11) | copy-start | bytes 4718596
  22.3 1.8 %copy-start = (f32[4,2,256,256]{3,2,1,0:T(8,128)S(1)}, f32[4,2,256,256]{3,2,1,0:T(8,128)}, u32[]{:S(2)}) copy-start(f32[4,2,256,256]{3,2,1,0:T(8,128)} %refs_7_.1) | copy-start | bytes 6291460
  22.3 1.8 %copy-start.1 = (f32[2,256,256]{2,1,0:T(8,128)S(1)}, f32[2,256,256]{2,1,0:T(8,128)}, u32[]{:S(2)}) copy-start(f32[2,256,256]{2,1,0:T(8,128)} %refs_0_.1) | copy-start | bytes 1572868
  22.4 1.9 %copy-start.2 = (bf16[4,256,256]{2,1,0:T(8,128)(2,1)S(1)}, bf16[4,256,256]{2,1,0:T(8,128)(2,1)}, u32[]{:S(2)}) copy-start(bf16[4,256,256]{2,1,0:T(8,128)(2,1)} %constant.7.clone.refs_8_.refs_9_) | copy-start | bytes 1572868
  39.6 9.0 %collective-permute-start.6 = (f32[256,256]{1,0:T(8,128)S(1)}, f32[256,256]{1,0:T(8,128)S(1)}, u32[]{:S(2)}, u32[]{:S(2)}) collective-permute-start(f32[256,256]{1,0:T(8,128)S(1)} %get-tuple-element.22), channel_id=1, source_target_pairs={{0,1},{1,2},{2,3},{3,4},{4,5},{5,6},{6,7},{7,8},{8,9},{9,10},{10,1... | collective-permute-start | bytes 786440 | tf_op jit(solution)/shard_map/ppermute | solution.py:32
  44.7 7.7 %collective-permute-start.8 = (f32[256,256]{1,0:T(8,128)S(1)}, f32[256,256]{1,0:T(8,128)S(1)}, u32[]{:S(2)}, u32[]{:S(2)}) collective-permute-start(f32[256,256]{1,0:T(8,128)S(1)} %get-tuple-element.25), channel_id=1, source_target_pairs={{0,1},{1,2},{2,3},{3,4},{4,5},{5,6},{6,7},{7,8},{8,9},{9,10},{10,1... | collective-permute-start | bytes 786440 | tf_op jit(solution)/shard_map/ppermute | solution.py:32
  46.7 20.1 %collective-permute-start.5 = (f32[2,256,256]{2,1,0:T(8,128)S(1)}, f32[2,256,256]{2,1,0:T(8,128)S(1)}, u32[]{:S(2)}, u32[]{:S(2)}) collective-permute-start(f32[2,256,256]{2,1,0:T(8,128)S(1)} %get-tuple-element.20), channel_id=1, source_target_pairs={{0,1},{1,2},{2,3},{3,4},{4,5},{5,6},{6,7},{7,8},{8,9},{9,10},{10,1... | collective-permute-start | bytes 1572872 | tf_op jit(solution)/shard_map/ppermute | solution.py:32
  48.6 13.1 %collective-permute-start.7 = (f32[256,256]{1,0:T(8,128)S(1)}, f32[256,256]{1,0:T(8,128)S(1)}, u32[]{:S(2)}, u32[]{:S(2)}) collective-permute-start(f32[256,256]{1,0:T(8,128)S(1)} %add.37), channel_id=1, source_target_pairs={{0,16},{16,32},{32,48},{48,64},{64,80},{80,96},{96,112},{1,17},{17... | collective-permute-start | bytes 786440 | tf_op jit(solution)/shard_map/ppermute | solution.py:32
  52.5 14.3 %collective-permute-start.9 = (f32[256,256]{1,0:T(8,128)S(1)}, f32[256,256]{1,0:T(8,128)S(1)}, u32[]{:S(2)}, u32[]{:S(2)}) collective-permute-start(f32[256,256]{1,0:T(8,128)S(1)} %add.40), channel_id=1, source_target_pairs={{0,16},{16,32},{32,48},{48,64},{64,80},{80,96},{96,112},{1,17},{17... | collective-permute-start | bytes 786440 | tf_op jit(solution)/shard_map/ppermute | solution.py:32
  66.9 9.6 %collective-permute-start.12 = (f32[256,256]{1,0:T(8,128)S(1)}, f32[256,256]{1,0:T(8,128)S(1)}, u32[]{:S(2)}, u32[]{:S(2)}) collective-permute-start(f32[256,256]{1,0:T(8,128)S(1)} %get-tuple-element.34.refs_1_), channel_id=1, source_target_pairs={{16,0},{32,16},{48,32},{64,48},{80,64},{96,80},{112,96},{17,1},{33... | collective-permute-start | bytes 786440 | tf_op jit(solution)/shard_map/ppermute | solution.py:32
  70.6 15.9 %collective-permute-start.10 = (f32[2,256,256]{2,1,0:T(8,128)S(1)}, f32[2,256,256]{2,1,0:T(8,128)S(1)}, u32[]{:S(2)}, u32[]{:S(2)}) collective-permute-start(f32[2,256,256]{2,1,0:T(8,128)S(1)} %pad_maximum_fusion), channel_id=1, source_target_pairs={{1,0},{2,1},{3,2},{4,3},{5,4},{6,5},{7,6},{8,7},{9,8},{10,9},{11,1... | collective-permute-start | bytes 1572872 | tf_op jit(solution)/shard_map/ppermute | solution.py:32
  73.1 10.0 %collective-permute-start.11 = (f32[256,256]{1,0:T(8,128)S(1)}, f32[256,256]{1,0:T(8,128)S(1)}, u32[]{:S(2)}, u32[]{:S(2)}) collective-permute-start(f32[256,256]{1,0:T(8,128)S(1)} %get-tuple-element.33.refs_0_), channel_id=1, source_target_pairs={{16,0},{32,16},{48,32},{64,48},{80,64},{96,80},{112,96},{17,1},{33... | collective-permute-start | bytes 786440 | tf_op jit(solution)/shard_map/ppermute | solution.py:32
  76.5 10.0 %collective-permute-start.14 = (f32[256,256]{1,0:T(8,128)S(1)}, f32[256,256]{1,0:T(8,128)S(1)}, u32[]{:S(2)}, u32[]{:S(2)}) collective-permute-start(f32[256,256]{1,0:T(8,128)S(1)} %collective-permute-done.12.refs_4_), channel_id=1, source_target_pairs={{1,0},{2,1},{3,2},{4,3},{5,4},{6,5},{7,6},{8,7},{9,8},{10,9},{11,1... | collective-permute-start | bytes 786440 | tf_op jit(solution)/shard_map/ppermute | solution.py:32
  83.1 7.2 %collective-permute-start.13 = (f32[256,256]{1,0:T(8,128)S(1)}, f32[256,256]{1,0:T(8,128)S(1)}, u32[]{:S(2)}, u32[]{:S(2)}) collective-permute-start(f32[256,256]{1,0:T(8,128)S(1)} %collective-permute-done.11.refs_3_), channel_id=1, source_target_pairs={{1,0},{2,1},{3,2},{4,3},{5,4},{6,5},{7,6},{8,7},{9,8},{10,9},{11,1... | collective-permute-start | bytes 786440 | tf_op jit(solution)/shard_map/ppermute | solution.py:32
  105.7 8.9 %collective-permute-start.16 = (f32[256,256]{1,0:T(8,128)S(1)}, f32[256,256]{1,0:T(8,128)S(1)}, u32[]{:S(2)}, u32[]{:S(2)}) collective-permute-start(f32[256,256]{1,0:T(8,128)S(1)} %get-tuple-element.29), channel_id=1, source_target_pairs={{0,1},{1,2},{2,3},{3,4},{4,5},{5,6},{6,7},{7,8},{8,9},{9,10},{10,1... | collective-permute-start | bytes 786440 | tf_op jit(solution)/shard_map/ppermute | solution.py:32
  110.7 7.7 %collective-permute-start.18 = (f32[256,256]{1,0:T(8,128)S(1)}, f32[256,256]{1,0:T(8,128)S(1)}, u32[]{:S(2)}, u32[]{:S(2)}) collective-permute-start(f32[256,256]{1,0:T(8,128)S(1)} %get-tuple-element.32), channel_id=1, source_target_pairs={{0,1},{1,2},{2,3},{3,4},{4,5},{5,6},{6,7},{7,8},{8,9},{9,10},{10,1... | collective-permute-start | bytes 786440 | tf_op jit(solution)/shard_map/ppermute | solution.py:32
  112.7 19.8 %collective-permute-start.15 = (f32[2,256,256]{2,1,0:T(8,128)S(1)}, f32[2,256,256]{2,1,0:T(8,128)S(1)}, u32[]{:S(2)}, u32[]{:S(2)}) collective-permute-start(f32[2,256,256]{2,1,0:T(8,128)S(1)} %get-tuple-element.27), channel_id=1, source_target_pairs={{0,1},{1,2},{2,3},{3,4},{4,5},{5,6},{6,7},{7,8},{8,9},{9,10},{10,1... | collective-permute-start | bytes 1572872 | tf_op jit(solution)/shard_map/ppermute | solution.py:32
  114.7 13.2 %collective-permute-start.17 = (f32[256,256]{1,0:T(8,128)S(1)}, f32[256,256]{1,0:T(8,128)S(1)}, u32[]{:S(2)}, u32[]{:S(2)}) collective-permute-start(f32[256,256]{1,0:T(8,128)S(1)} %add.43), channel_id=1, source_target_pairs={{0,16},{16,32},{32,48},{48,64},{64,80},{80,96},{96,112},{1,17},{17... | collective-permute-start | bytes 786440 | tf_op jit(solution)/shard_map/ppermute | solution.py:32
  118.5 14.0 %collective-permute-start.19 = (f32[256,256]{1,0:T(8,128)S(1)}, f32[256,256]{1,0:T(8,128)S(1)}, u32[]{:S(2)}, u32[]{:S(2)}) collective-permute-start(f32[256,256]{1,0:T(8,128)S(1)} %add.46), channel_id=1, source_target_pairs={{0,16},{16,32},{32,48},{48,64},{64,80},{80,96},{96,112},{1,17},{17... | collective-permute-start | bytes 786440 | tf_op jit(solution)/shard_map/ppermute | solution.py:32
  (1 other events, 0.9 us)

commit v3 on v2

--- a/solution.py
+++ b/solution.py
@@ -27,9 +27,8 @@
 
 
 def from_behind(block, axis, distance):
-    devices = range(lax.axis_size(axis))
-    route = [(i - distance, i) for i in devices if i - distance in devices]
-    return lax.ppermute(block, axis, route)
+    size = lax.axis_size(axis)
+    return lax.ppermute(block, axis, [(i, (i + distance) % size) for i in range(size)])
 
 
 def tables():
@@ -123,8 +122,16 @@
     outs, scratch = refs[: len(out_at)], refs[len(out_at) :]
     left_ext, right_ext, left_sum, right_sum, patch, far, chis, grad = scratch
     modes = probe_ref.shape[0]
+    row_inside = lax.axis_index("row") < lax.axis_size("row") - 1
+    col_inside = lax.axis_index("col") < lax.axis_size("col") - 1
+
+    def masked(values, half, at):
+        if half:
+            values = jnp.where(col_inside, values, 0.0)
+        return jnp.where(row_inside, values, 0.0) if at.start else values
+
     for tile, (half, part, at) in zip(tiles, tile_at):
-        (left_ext, right_ext)[half][part, at] = tile[...]
+        (left_ext, right_ext)[half][part, at] = masked(tile[...], half, at)
     left_sum[...] = jnp.zeros_like(left_sum)
     right_sum[...] = jnp.zeros_like(right_sum)
     groups = SIDE // SUB
@@ -224,7 +231,7 @@
 
     lax.fori_loop(0, count_ref[0, 0], position, 0)
     for out, (half, part, at) in zip(outs, out_at):
-        out[...] = (left_sum, right_sum)[half][part, at]
+        out[...] = masked((left_sum, right_sum)[half][part, at], half, at)
 
 
 def gradient(offsets, count, own, right, below, diag, probe, amplitude, table, out_splits):

time: 134 us -> 134 us (level)
  the two profiles are of different devices: /device:TPU:38 before, /device:TPU:0 now
where the time goes in v3:
time: 134 us
  waiting for transfers between devices  77.1 us (58%)
  starting transfers between devices  37.5 us (28%)
  Pallas kernels  13.4 us (10%)
  local copies, waits for them, and re-layouts  4.15 us (3%)
    ppermute x20, waiting for transfers between devices, from_behind(): lax.ppermute(block, axis, [(i, (i + distance) % size) for i in range(size)])  77.1 us
    ppermute x20, starting transfers between devices, from_behind(): lax.ppermute(block, axis, [(i, (i + distance) % size) for i in range(size)])  37.5 us
    pallas_call x2, Pallas kernels, gradient(): pl.pallas_call(functools.partial(update_kernel, in_splits, out_splits), o...  11.6 us
    unnamed x11, local copies, waits for them, and re-layouts  3.09 us
  transfers between devices with their start and end apart: 20, of which 14 were waited for; matrix products, arithmetic and copies ran while one was open for 1% of the time, Pallas kernels for 1%

profile of v3, /device:TPU:0, one launch (start us, length us, event | category | flops | bytes accessed | tf_op | source)
XLA Modules:
  0.0 134.3 jit_solution(10475007002278370480)
XLA Ops:
  1.1 4.5 %collective-permute-start.2 = (f32[256,256]{1,0:T(8,128)S(1)}, f32[256,256]{1,0:T(8,128)S(1)}, u32[]{:S(2)}, u32[]{:S(2)}) collective-permute-start(f32[256,256]{1,0:T(8,128)S(1)} %get-tuple-element.37), channel_id=1, source_target_pairs={{0,112},{16,0},{32,16},{48,32},{64,48},{80,64},{96,80},{112,96},{1... | collective-permute-start | bytes 786440 | tf_op jit(solution)/shard_map/ppermute | solution.py:31
  6.3 4.7 %collective-permute-start = (f32[2,256,256]{2,1,0:T(8,128)}, f32[2,256,256]{2,1,0:T(8,128)S(1)}, u32[]{:S(2)}, u32[]{:S(2)}) collective-permute-start(f32[2,256,256]{2,1,0:T(8,128)} %refs_0_.1), channel_id=1, source_target_pairs={{0,15},{1,0},{2,1},{3,2},{4,3},{5,4},{6,5},{7,6},{8,7},{9,8},{10,9... | collective-permute-start | bytes 1572872 | tf_op jit(solution)/shard_map/ppermute | solution.py:31
  11.0 1.3 collective-permute-done.2.refs_3_
  12.3 5.4 %collective-permute-start.4 = (f32[256,256]{1,0:T(8,128)S(1)}, f32[256,256]{1,0:T(8,128)S(1)}, u32[]{:S(2)}, u32[]{:S(2)}) collective-permute-start(f32[256,256]{1,0:T(8,128)S(1)} %collective-permute-done.2.refs_3_), channel_id=1, source_target_pairs={{0,15},{1,0},{2,1},{3,2},{4,3},{5,4},{6,5},{7,6},{8,7},{9,8},{10,9... | collective-permute-start | bytes 786440 | tf_op jit(solution)/shard_map/ppermute | solution.py:31
  17.7 11.2 %collective-permute-start.3 = (f32[256,256]{1,0:T(8,128)S(1)}, f32[256,256]{1,0:T(8,128)S(1)}, u32[]{:S(2)}, u32[]{:S(2)}) collective-permute-start(f32[256,256]{1,0:T(8,128)S(1)} %collective-permute-done.1.refs_2_), channel_id=1, source_target_pairs={{0,15},{1,0},{2,1},{3,2},{4,3},{5,4},{6,5},{7,6},{8,7},{9,8},{10,9... | collective-permute-start | bytes 786440 | tf_op jit(solution)/shard_map/ppermute | solution.py:31
  30.4 1.4 %copy-done.3 = f32[1,1,6,256,256]{4,3,2,1,0:T(8,128)S(1)} copy-done((f32[1,1,6,256,256]{4,3,2,1,0:T(8,128)S(1)}, f32[1,1,6,256,256]{4,3,2,1,0:T(8,128)}, u32[]{:S(2)}) %copy-start.3) | copy-done | bytes 1572888
  32.7 1.8 %shard_map.73.refs_7_.refs_8_ = f32[6,256,256]{2,1,0:T(8,128)S(1)} custom-call(bf16[256,256]{1,0:T(8,128)(2,1)S(1)} %copy-done.4, f32[6,256,256]{2,1,0:T(8,128)S(1)} %bitcast.55), custom_call_target="tpu_custom_call" | custom-call | flops 603979776 | bytes 3145728 | tf_op jit(solution)/shard_map/pallas_call | solution.py:75
  34.5 5.8 %shard_map.74 = (f32[256,256]{1,0:T(8,128)S(1)}, f32[256,256]{1,0:T(8,128)S(1)}, f32[2,256,256]{2,1,0:T(8,128)S(1)}, f32[256,256]{1,0:T(8,128)S(1)}, f32[256,256...) custom-call(s32[1,1,6,2]{3,2,1,0:T(8,128)S(1)} %copy.8.offsets_ref, s32[1,1]{1,0:T(1,128)S(6)} %copy.10.count_ref, ...), custom_call_target="tpu_custom_call" | custom-call | tf_op jit(solution)/shard_map/pallas_call | solution.py:245
  40.6 13.0 %collective-permute-done.6 = f32[256,256]{1,0:T(8,128)S(1)} collective-permute-done((f32[256,256]{1,0:T(8,128)S(1)}, f32[256,256]{1,0:T(8,128)S(1)}, u32[]{:S(2)}, u32[]{:S(2)}) %collective-permute-start.6) | collective-permute-done | bytes 262176 | tf_op jit(solution)/shard_map/ppermute | solution.py:31
  53.7 5.5 %collective-permute-done.8 = f32[256,256]{1,0:T(8,128)S(1)} collective-permute-done((f32[256,256]{1,0:T(8,128)S(1)}, f32[256,256]{1,0:T(8,128)S(1)}, u32[]{:S(2)}, u32[]{:S(2)}) %collective-permute-start.8) | collective-permute-done | bytes 262176 | tf_op jit(solution)/shard_map/ppermute | solution.py:31
  59.3 4.6 %collective-permute-done.7 = f32[256,256]{1,0:T(8,128)S(1)} collective-permute-done((f32[256,256]{1,0:T(8,128)S(1)}, f32[256,256]{1,0:T(8,128)S(1)}, u32[]{:S(2)}, u32[]{:S(2)}) %collective-permute-start.7) | collective-permute-done | bytes 262176 | tf_op jit(solution)/shard_map/ppermute | solution.py:31
  63.9 3.9 %collective-permute-done.9 = f32[256,256]{1,0:T(8,128)S(1)} collective-permute-done((f32[256,256]{1,0:T(8,128)S(1)}, f32[256,256]{1,0:T(8,128)S(1)}, u32[]{:S(2)}, u32[]{:S(2)}) %collective-permute-start.9) | collective-permute-done | bytes 262176 | tf_op jit(solution)/shard_map/ppermute | solution.py:31
  67.8 2.6 %collective-permute-done.5 = f32[2,256,256]{2,1,0:T(8,128)S(1)} collective-permute-done((f32[2,256,256]{2,1,0:T(8,128)S(1)}, f32[2,256,256]{2,1,0:T(8,128)S(1)}, u32[]{:S(2)}, u32[]{:S(2)}) %collective-permute-start.5) | collective-permute-done | bytes 524320 | tf_op jit(solution)/shard_map/ppermute | solution.py:31
  70.7 1.2 collective-permute-start.10
  71.9 7.8 %collective-permute-done.12.refs_4_ = f32[256,256]{1,0:T(8,128)S(1)} collective-permute-done((f32[256,256]{1,0:T(8,128)S(1)}, f32[256,256]{1,0:T(8,128)S(1)}, u32[]{:S(2)}, u32[]{:S(2)}) %collective-permute-start.12) | collective-permute-done | bytes 262176 | tf_op jit(solution)/shard_map/ppermute | solution.py:31
  79.8 2.8 %collective-permute-done.11.refs_3_ = f32[256,256]{1,0:T(8,128)S(1)} collective-permute-done((f32[256,256]{1,0:T(8,128)S(1)}, f32[256,256]{1,0:T(8,128)S(1)}, u32[]{:S(2)}, u32[]{:S(2)}) %collective-permute-start.11) | collective-permute-done | bytes 262176 | tf_op jit(solution)/shard_map/ppermute | solution.py:31
  82.6 8.0 %collective-permute-start.13 = (f32[256,256]{1,0:T(8,128)S(1)}, f32[256,256]{1,0:T(8,128)S(1)}, u32[]{:S(2)}, u32[]{:S(2)}) collective-permute-start(f32[256,256]{1,0:T(8,128)S(1)} %collective-permute-done.11.refs_3_), channel_id=1, source_target_pairs={{0,15},{1,0},{2,1},{3,2},{4,3},{5,4},{6,5},{7,6},{8,7},{9,8},{10,9... | collective-permute-start | bytes 786440 | tf_op jit(solution)/shard_map/ppermute | solution.py:31
  90.6 3.9 %collective-permute-done.13.refs_5_ = f32[256,256]{1,0:T(8,128)S(1)} collective-permute-done((f32[256,256]{1,0:T(8,128)S(1)}, f32[256,256]{1,0:T(8,128)S(1)}, u32[]{:S(2)}, u32[]{:S(2)}) %collective-permute-start.13) | collective-permute-done | bytes 262176 | tf_op jit(solution)/shard_map/ppermute | solution.py:31
  94.5 5.8 %shard_map.75 = (f32[256,256]{1,0:T(8,128)S(1)}, f32[256,256]{1,0:T(8,128)S(1)}, f32[2,256,256]{2,1,0:T(8,128)S(1)}, f32[256,256]{1,0:T(8,128)S(1)}, f32[256,256...) custom-call(s32[1,1,6,2]{3,2,1,0:T(8,128)S(1)} %copy.8.offsets_ref, s32[1,1]{1,0:T(1,128)S(6)} %copy.10.count_ref, ...), custom_call_target="tpu_custom_call" | custom-call | tf_op jit(solution)/shard_map/pallas_call | solution.py:245
  101.4 15.1 %collective-permute-done.16 = f32[256,256]{1,0:T(8,128)S(1)} collective-permute-done((f32[256,256]{1,0:T(8,128)S(1)}, f32[256,256]{1,0:T(8,128)S(1)}, u32[]{:S(2)}, u32[]{:S(2)}) %collective-permute-start.16) | collective-permute-done | bytes 262176 | tf_op jit(solution)/shard_map/ppermute | solution.py:31
  116.6 5.5 %collective-permute-done.18 = f32[256,256]{1,0:T(8,128)S(1)} collective-permute-done((f32[256,256]{1,0:T(8,128)S(1)}, f32[256,256]{1,0:T(8,128)S(1)}, u32[]{:S(2)}, u32[]{:S(2)}) %collective-permute-start.18) | collective-permute-done | bytes 262176 | tf_op jit(solution)/shard_map/ppermute | solution.py:31
  122.2 4.2 %collective-permute-done.17 = f32[256,256]{1,0:T(8,128)S(1)} collective-permute-done((f32[256,256]{1,0:T(8,128)S(1)}, f32[256,256]{1,0:T(8,128)S(1)}, u32[]{:S(2)}, u32[]{:S(2)}) %collective-permute-start.17) | collective-permute-done | bytes 262176 | tf_op jit(solution)/shard_map/ppermute | solution.py:31
  126.4 4.2 %collective-permute-done.19 = f32[256,256]{1,0:T(8,128)S(1)} collective-permute-done((f32[256,256]{1,0:T(8,128)S(1)}, f32[256,256]{1,0:T(8,128)S(1)}, u32[]{:S(2)}, u32[]{:S(2)}) %collective-permute-start.19) | collective-permute-done | bytes 262176 | tf_op jit(solution)/shard_map/ppermute | solution.py:31
  130.7 2.6 %collective-permute-done.15 = f32[2,256,256]{2,1,0:T(8,128)S(1)} collective-permute-done((f32[2,256,256]{2,1,0:T(8,128)S(1)}, f32[2,256,256]{2,1,0:T(8,128)S(1)}, u32[]{:S(2)}, u32[]{:S(2)}) %collective-permute-start.15) | collective-permute-done | bytes 524320 | tf_op jit(solution)/shard_map/ppermute | solution.py:31
  (39 shorter events, 6.6 us)
Async XLA Ops:
  1.1 11.2 %collective-permute-start.2 = (f32[256,256]{1,0:T(8,128)S(1)}, f32[256,256]{1,0:T(8,128)S(1)}, u32[]{:S(2)}, u32[]{:S(2)}) collective-permute-start(f32[256,256]{1,0:T(8,128)S(1)} %get-tuple-element.37), channel_id=1, source_target_pairs={{0,112},{16,0},{32,16},{48,32},{64,48},{80,64},{96,80},{112,96},{1... | collective-permute-start | bytes 786440 | tf_op jit(solution)/shard_map/ppermute | solution.py:31
  5.6 12.2 %collective-permute-start.1 = (f32[256,256]{1,0:T(8,128)S(1)}, f32[256,256]{1,0:T(8,128)S(1)}, u32[]{:S(2)}, u32[]{:S(2)}) collective-permute-start(f32[256,256]{1,0:T(8,128)S(1)} %get-tuple-element.38), channel_id=1, source_target_pairs={{0,112},{16,0},{32,16},{48,32},{64,48},{80,64},{96,80},{112,96},{1... | collective-permute-start | bytes 786440 | tf_op jit(solution)/shard_map/ppermute | solution.py:31
  6.3 28.2 %collective-permute-start = (f32[2,256,256]{2,1,0:T(8,128)}, f32[2,256,256]{2,1,0:T(8,128)S(1)}, u32[]{:S(2)}, u32[]{:S(2)}) collective-permute-start(f32[2,256,256]{2,1,0:T(8,128)} %refs_0_.1), channel_id=1, source_target_pairs={{0,15},{1,0},{2,1},{3,2},{4,3},{5,4},{6,5},{7,6},{8,7},{9,8},{10,9... | collective-permute-start | bytes 1572872 | tf_op jit(solution)/shard_map/ppermute | solution.py:31
  12.3 22.2 %collective-permute-start.4 = (f32[256,256]{1,0:T(8,128)S(1)}, f32[256,256]{1,0:T(8,128)S(1)}, u32[]{:S(2)}, u32[]{:S(2)}) collective-permute-start(f32[256,256]{1,0:T(8,128)S(1)} %collective-permute-done.2.refs_3_), channel_id=1, source_target_pairs={{0,15},{1,0},{2,1},{3,2},{4,3},{5,4},{6,5},{7,6},{8,7},{9,8},{10,9... | collective-permute-start | bytes 786440 | tf_op jit(solution)/shard_map/ppermute | solution.py:31
  17.7 16.7 %collective-permute-start.3 = (f32[256,256]{1,0:T(8,128)S(1)}, f32[256,256]{1,0:T(8,128)S(1)}, u32[]{:S(2)}, u32[]{:S(2)}) collective-permute-start(f32[256,256]{1,0:T(8,128)S(1)} %collective-permute-done.1.refs_2_), channel_id=1, source_target_pairs={{0,15},{1,0},{2,1},{3,2},{4,3},{5,4},{6,5},{7,6},{8,7},{9,8},{10,9... | collective-permute-start | bytes 786440 | tf_op jit(solution)/shard_map/ppermute | solution.py:31
  30.4 1.4 %copy-start.3 = (f32[1,1,6,256,256]{4,3,2,1,0:T(8,128)S(1)}, f32[1,1,6,256,256]{4,3,2,1,0:T(8,128)}, u32[]{:S(2)}) copy-start(f32[1,1,6,256,256]{4,3,2,1,0:T(8,128)} %param.11) | copy-start | bytes 4718596
  32.7 1.8 %copy-start = (f32[4,2,256,256]{3,2,1,0:T(8,128)S(1)}, f32[4,2,256,256]{3,2,1,0:T(8,128)}, u32[]{:S(2)}) copy-start(f32[4,2,256,256]{3,2,1,0:T(8,128)} %refs_7_.1) | copy-start | bytes 6291460
  32.7 1.8 %copy-start.1 = (f32[2,256,256]{2,1,0:T(8,128)S(1)}, f32[2,256,256]{2,1,0:T(8,128)}, u32[]{:S(2)}) copy-start(f32[2,256,256]{2,1,0:T(8,128)} %refs_0_.1) | copy-start | bytes 1572868
  32.7 1.9 %copy-start.2 = (bf16[4,256,256]{2,1,0:T(8,128)(2,1)S(1)}, bf16[4,256,256]{2,1,0:T(8,128)(2,1)}, u32[]{:S(2)}) copy-start(bf16[4,256,256]{2,1,0:T(8,128)(2,1)} %constant.7.clone.refs_8_.refs_9_) | copy-start | bytes 1572868
  40.3 13.2 %collective-permute-start.6 = (f32[256,256]{1,0:T(8,128)S(1)}, f32[256,256]{1,0:T(8,128)S(1)}, u32[]{:S(2)}, u32[]{:S(2)}) collective-permute-start(f32[256,256]{1,0:T(8,128)S(1)} %get-tuple-element.22), channel_id=1, source_target_pairs={{0,1},{1,2},{2,3},{3,4},{4,5},{5,6},{6,7},{7,8},{8,9},{9,10},{10,1... | collective-permute-start | bytes 786440 | tf_op jit(solution)/shard_map/ppermute | solution.py:31
  40.4 18.8 %collective-permute-start.8 = (f32[256,256]{1,0:T(8,128)S(1)}, f32[256,256]{1,0:T(8,128)S(1)}, u32[]{:S(2)}, u32[]{:S(2)}) collective-permute-start(f32[256,256]{1,0:T(8,128)S(1)} %get-tuple-element.25), channel_id=1, source_target_pairs={{0,1},{1,2},{2,3},{3,4},{4,5},{5,6},{6,7},{7,8},{8,9},{9,10},{10,1... | collective-permute-start | bytes 786440 | tf_op jit(solution)/shard_map/ppermute | solution.py:31
  40.5 29.9 %collective-permute-start.5 = (f32[2,256,256]{2,1,0:T(8,128)S(1)}, f32[2,256,256]{2,1,0:T(8,128)S(1)}, u32[]{:S(2)}, u32[]{:S(2)}) collective-permute-start(f32[2,256,256]{2,1,0:T(8,128)S(1)} %get-tuple-element.20), channel_id=1, source_target_pairs={{0,1},{1,2},{2,3},{3,4},{4,5},{5,6},{6,7},{7,8},{8,9},{9,10},{10,1... | collective-permute-start | bytes 1572872 | tf_op jit(solution)/shard_map/ppermute | solution.py:31
  53.6 10.3 %collective-permute-start.7 = (f32[256,256]{1,0:T(8,128)S(1)}, f32[256,256]{1,0:T(8,128)S(1)}, u32[]{:S(2)}, u32[]{:S(2)}) collective-permute-start(f32[256,256]{1,0:T(8,128)S(1)} %add.37), channel_id=1, source_target_pairs={{0,16},{16,32},{32,48},{48,64},{64,80},{80,96},{96,112},{112,0},{1... | collective-permute-start | bytes 786440 | tf_op jit(solution)/shard_map/ppermute | solution.py:31
  59.2 8.6 %collective-permute-start.9 = (f32[256,256]{1,0:T(8,128)S(1)}, f32[256,256]{1,0:T(8,128)S(1)}, u32[]{:S(2)}, u32[]{:S(2)}) collective-permute-start(f32[256,256]{1,0:T(8,128)S(1)} %add.40), channel_id=1, source_target_pairs={{0,16},{16,32},{32,48},{48,64},{64,80},{80,96},{96,112},{112,0},{1... | collective-permute-start | bytes 786440 | tf_op jit(solution)/shard_map/ppermute | solution.py:31
  70.6 9.2 %collective-permute-start.12 = (f32[256,256]{1,0:T(8,128)S(1)}, f32[256,256]{1,0:T(8,128)S(1)}, u32[]{:S(2)}, u32[]{:S(2)}) collective-permute-start(f32[256,256]{1,0:T(8,128)S(1)} %get-tuple-element.34.refs_1_), channel_id=1, source_target_pairs={{0,112},{16,0},{32,16},{48,32},{64,48},{80,64},{96,80},{112,96},{1... | collective-permute-start | bytes 786440 | tf_op jit(solution)/shard_map/ppermute | solution.py:31
  70.7 19.9 %collective-permute-start.10 = (f32[2,256,256]{2,1,0:T(8,128)S(1)}, f32[2,256,256]{2,1,0:T(8,128)S(1)}, u32[]{:S(2)}, u32[]{:S(2)}) collective-permute-start(f32[2,256,256]{2,1,0:T(8,128)S(1)} %pad_maximum_fusion), channel_id=1, source_target_pairs={{0,15},{1,0},{2,1},{3,2},{4,3},{5,4},{6,5},{7,6},{8,7},{9,8},{10,9... | collective-permute-start | bytes 1572872 | tf_op jit(solution)/shard_map/ppermute | solution.py:31
  71.9 10.6 %collective-permute-start.11 = (f32[256,256]{1,0:T(8,128)S(1)}, f32[256,256]{1,0:T(8,128)S(1)}, u32[]{:S(2)}, u32[]{:S(2)}) collective-permute-start(f32[256,256]{1,0:T(8,128)S(1)} %get-tuple-element.33.refs_0_), channel_id=1, source_target_pairs={{0,112},{16,0},{32,16},{48,32},{64,48},{80,64},{96,80},{112,96},{1... | collective-permute-start | bytes 786440 | tf_op jit(solution)/shard_map/ppermute | solution.py:31
  79.8 10.8 %collective-permute-start.14 = (f32[256,256]{1,0:T(8,128)S(1)}, f32[256,256]{1,0:T(8,128)S(1)}, u32[]{:S(2)}, u32[]{:S(2)}) collective-permute-start(f32[256,256]{1,0:T(8,128)S(1)} %collective-permute-done.12.refs_4_), channel_id=1, source_target_pairs={{0,15},{1,0},{2,1},{3,2},{4,3},{5,4},{6,5},{7,6},{8,7},{9,8},{10,9... | collective-permute-start | bytes 786440 | tf_op jit(solution)/shard_map/ppermute | solution.py:31
  82.6 11.9 %collective-permute-start.13 = (f32[256,256]{1,0:T(8,128)S(1)}, f32[256,256]{1,0:T(8,128)S(1)}, u32[]{:S(2)}, u32[]{:S(2)}) collective-permute-start(f32[256,256]{1,0:T(8,128)S(1)} %collective-permute-done.11.refs_3_), channel_id=1, source_target_pairs={{0,15},{1,0},{2,1},{3,2},{4,3},{5,4},{6,5},{7,6},{8,7},{9,8},{10,9... | collective-permute-start | bytes 786440 | tf_op jit(solution)/shard_map/ppermute | solution.py:31
  100.3 16.2 %collective-permute-start.16 = (f32[256,256]{1,0:T(8,128)S(1)}, f32[256,256]{1,0:T(8,128)S(1)}, u32[]{:S(2)}, u32[]{:S(2)}) collective-permute-start(f32[256,256]{1,0:T(8,128)S(1)} %get-tuple-element.29), channel_id=1, source_target_pairs={{0,1},{1,2},{2,3},{3,4},{4,5},{5,6},{6,7},{7,8},{8,9},{9,10},{10,1... | collective-permute-start | bytes 786440 | tf_op jit(solution)/shard_map/ppermute | solution.py:31
  100.4 21.7 %collective-permute-start.18 = (f32[256,256]{1,0:T(8,128)S(1)}, f32[256,256]{1,0:T(8,128)S(1)}, u32[]{:S(2)}, u32[]{:S(2)}) collective-permute-start(f32[256,256]{1,0:T(8,128)S(1)} %get-tuple-element.32), channel_id=1, source_target_pairs={{0,1},{1,2},{2,3},{3,4},{4,5},{5,6},{6,7},{7,8},{8,9},{9,10},{10,1... | collective-permute-start | bytes 786440 | tf_op jit(solution)/shard_map/ppermute | solution.py:31
  101.3 32.0 %collective-permute-start.15 = (f32[2,256,256]{2,1,0:T(8,128)S(1)}, f32[2,256,256]{2,1,0:T(8,128)S(1)}, u32[]{:S(2)}, u32[]{:S(2)}) collective-permute-start(f32[2,256,256]{2,1,0:T(8,128)S(1)} %get-tuple-element.27), channel_id=1, source_target_pairs={{0,1},{1,2},{2,3},{3,4},{4,5},{5,6},{6,7},{7,8},{8,9},{9,10},{10,1... | collective-permute-start | bytes 1572872 | tf_op jit(solution)/shard_map/ppermute | solution.py:31
  116.5 9.9 %collective-permute-start.17 = (f32[256,256]{1,0:T(8,128)S(1)}, f32[256,256]{1,0:T(8,128)S(1)}, u32[]{:S(2)}, u32[]{:S(2)}) collective-permute-start(f32[256,256]{1,0:T(8,128)S(1)} %add.43), channel_id=1, source_target_pairs={{0,16},{16,32},{32,48},{48,64},{64,80},{80,96},{96,112},{112,0},{1... | collective-permute-start | bytes 786440 | tf_op jit(solution)/shard_map/ppermute | solution.py:31
  122.1 8.6 %collective-permute-start.19 = (f32[256,256]{1,0:T(8,128)S(1)}, f32[256,256]{1,0:T(8,128)S(1)}, u32[]{:S(2)}, u32[]{:S(2)}) collective-permute-start(f32[256,256]{1,0:T(8,128)S(1)} %add.46), channel_id=1, source_target_pairs={{0,16},{16,32},{32,48},{48,64},{64,80},{80,96},{96,112},{112,0},{1... | collective-permute-start | bytes 786440 | tf_op jit(solution)/shard_map/ppermute | solution.py:31
  (1 other events, 0.9 us)

commit v4 on v3

--- a/solution.py
+++ b/solution.py
@@ -17,8 +17,9 @@
 HALF = 128
 SUB = 8
 CHUNK = 16
-H_SPLIT = [[False, False, True, True], [True, False, True, True]]
-G_SPLIT = [[True, False, True, True], [True, False, True, True]]
+CROSSED = (("col", -1), ("col", 1), ("row", -1))
+H_SPLIT = [[False, True, True, True], [True, True, True, True]]
+G_SPLIT = [[True, True, True, True], [True, True, True, True]]
 AHEAD = 1
 F32 = jnp.float32
 BF16 = jnp.bfloat16
@@ -27,8 +28,19 @@
 
 
 def from_behind(block, axis, distance):
-    size = lax.axis_size(axis)
-    return lax.ppermute(block, axis, [(i, (i + distance) % size) for i in range(size)])
+    sizes = {"row": lax.axis_size("row"), "col": lax.axis_size("col")}
+    route = []
+    for r in range(sizes["row"]):
+        for c in range(sizes["col"]):
+            to = {"row": r, "col": c}
+            to[axis] += distance
+            if not 0 <= to[axis] < sizes[axis]:
+                to[axis] %= sizes[axis]
+                other = "col" if axis == "row" else "row"
+                if (axis, distance) in CROSSED:
+                    to[other] = (to[other] + sizes[other] // 2) % sizes[other]
+            route.append((r * sizes["col"] + c, to["row"] * sizes["col"] + to["col"]))
+    return lax.ppermute(block, ("row", "col"), route)
 
 
 def tables():

time: 134 us -> 128 us (0.955); the launches traced: 134 us -> 126 us
  waiting for transfers between devices: 77.1 us -> 61.1 us
  Pallas kernels: 13.4 us -> 27.9 us
  starting transfers between devices: 37.5 us -> 30.4 us
    ppermute x20 -> x24, waiting for transfers between devices: 77.1 us -> 61.1 us  [from_behind(): return lax.ppermute(block, ('row', 'col'), route)]
    pallas_call x2, Pallas kernels: 11.6 us -> 26.1 us  [gradient(): pl.pallas_call(functools.partial(update_kernel, in_splits, out_splits), o...]
    ppermute x20 -> x24, starting transfers between devices: 37.5 us -> 30.4 us  [from_behind(): return lax.ppermute(block, ('row', 'col'), route)]
  transfers between devices with their start and end apart: 20 -> 24, of which waited for: 14 -> 15; matrix products, arithmetic and copies ran while one was open for 1% -> 1% of each run, Pallas kernels for 1% -> 1%
where the time goes in v4:
time: 128 us; the launch traced here: 126 us
  waiting for transfers between devices  61.1 us (48%)
  starting transfers between devices  30.4 us (24%)
  Pallas kernels  27.9 us (22%)
  local copies, waits for them, and re-layouts  4.15 us (3%)
    ppermute x24, waiting for transfers between devices, from_behind(): return lax.ppermute(block, ('row', 'col'), route)  61.1 us
    ppermute x24, starting transfers between devices, from_behind(): return lax.ppermute(block, ('row', 'col'), route)  30.4 us
    pallas_call x2, Pallas kernels, gradient(): pl.pallas_call(functools.partial(update_kernel, in_splits, out_splits), o...  26.1 us
    unnamed x11, local copies, waits for them, and re-layouts  3.09 us
  transfers between devices with their start and end apart: 24, of which 15 were waited for; matrix products, arithmetic and copies ran while one was open for 1% of the time, Pallas kernels for 1%

profile of v4, /device:TPU:0, one launch (start us, length us, event | category | flops | bytes accessed | tf_op | source)
XLA Modules:
  0.0 125.7 jit_solution(363034403676515083)
XLA Ops:
  1.1 6.6 %collective-permute-start.3 = (f32[256,256]{1,0:T(8,128)S(1)}, f32[256,256]{1,0:T(8,128)S(1)}, u32[]{:S(2)}, u32[]{:S(2)}) collective-permute-start(f32[256,256]{1,0:T(8,128)S(1)} %get-tuple-element.39), channel_id=1, source_target_pairs={{0,120},{1,121},{2,122},{3,123},{4,124},{5,125},{6,126},{7,127},{8... | collective-permute-start | bytes 786440 | tf_op jit(solution)/shard_map/ppermute | solution.py:43
  8.5 1.5 %collective-permute-start.1 = (f32[256,256]{1,0:T(8,128)S(1)}, f32[256,256]{1,0:T(8,128)S(1)}, u32[]{:S(2)}, u32[]{:S(2)}) collective-permute-start(f32[256,256]{1,0:T(8,128)S(1)} %get-tuple-element.39), channel_id=1, source_target_pairs={{0,79},{1,0},{2,1},{3,2},{4,3},{5,4},{6,5},{7,6},{8,7},{9,8},{10,9... | collective-permute-start | bytes 786440 | tf_op jit(solution)/shard_map/ppermute | solution.py:43
  11.2 3.3 %collective-permute-done.3.refs_4_ = f32[256,256]{1,0:T(8,128)S(1)} collective-permute-done((f32[256,256]{1,0:T(8,128)S(1)}, f32[256,256]{1,0:T(8,128)S(1)}, u32[]{:S(2)}, u32[]{:S(2)}) %collective-permute-start.3) | collective-permute-done | bytes 262176 | tf_op jit(solution)/shard_map/ppermute | solution.py:43
  15.3 3.6 %collective-permute-done.2.refs_3_ = f32[256,256]{1,0:T(8,128)S(1)} collective-permute-done((f32[256,256]{1,0:T(8,128)S(1)}, f32[256,256]{1,0:T(8,128)S(1)}, u32[]{:S(2)}, u32[]{:S(2)}) %collective-permute-start.2) | collective-permute-done | bytes 262176 | tf_op jit(solution)/shard_map/ppermute | solution.py:43
  18.9 7.6 %collective-permute-start.4 = (f32[256,256]{1,0:T(8,128)S(1)}, f32[256,256]{1,0:T(8,128)S(1)}, u32[]{:S(2)}, u32[]{:S(2)}) collective-permute-start(f32[256,256]{1,0:T(8,128)S(1)} %collective-permute-done.2.refs_3_), channel_id=1, source_target_pairs={{0,79},{1,0},{2,1},{3,2},{4,3},{5,4},{6,5},{7,6},{8,7},{9,8},{10,9... | collective-permute-start | bytes 786440 | tf_op jit(solution)/shard_map/ppermute | solution.py:43
  28.0 1.4 %copy-done.3 = f32[1,1,6,256,256]{4,3,2,1,0:T(8,128)S(1)} copy-done((f32[1,1,6,256,256]{4,3,2,1,0:T(8,128)S(1)}, f32[1,1,6,256,256]{4,3,2,1,0:T(8,128)}, u32[]{:S(2)}) %copy-start.3) | copy-done | bytes 1572888
  30.3 1.8 %shard_map.73.refs_8_.refs_9_ = f32[6,256,256]{2,1,0:T(8,128)S(1)} custom-call(bf16[256,256]{1,0:T(8,128)(2,1)S(1)} %copy-done.4, f32[6,256,256]{2,1,0:T(8,128)S(1)} %bitcast.11), custom_call_target="tpu_custom_call" | custom-call | flops 603979776 | bytes 3145728 | tf_op jit(solution)/shard_map/pallas_call | solution.py:87
  32.1 13.0 %shard_map.74 = (f32[256,256]{1,0:T(8,128)S(1)}, f32[256,256]{1,0:T(8,128)S(1)}, f32[256,256]{1,0:T(8,128)S(1)}, f32[256,256]{1,0:T(8,128)S(1)}, f32[256,256]{1,...) custom-call(s32[1,1,6,2]{3,2,1,0:T(8,128)S(1)} %copy.8.offsets_ref, ...), custom_call_target="tpu_custom_call" | custom-call | tf_op jit(solution)/shard_map/pallas_call | solution.py:257
  45.4 8.9 %collective-permute-done.7 = f32[256,256]{1,0:T(8,128)S(1)} collective-permute-done((f32[256,256]{1,0:T(8,128)S(1)}, f32[256,256]{1,0:T(8,128)S(1)}, u32[]{:S(2)}, u32[]{:S(2)}) %collective-permute-start.7) | collective-permute-done | bytes 262176 | tf_op jit(solution)/shard_map/ppermute | solution.py:43
  54.4 2.7 %collective-permute-done.10 = f32[256,256]{1,0:T(8,128)S(1)} collective-permute-done((f32[256,256]{1,0:T(8,128)S(1)}, f32[256,256]{1,0:T(8,128)S(1)}, u32[]{:S(2)}, u32[]{:S(2)}) %collective-permute-start.10) | collective-permute-done | bytes 262176 | tf_op jit(solution)/shard_map/ppermute | solution.py:43
  57.2 2.7 %collective-permute-done.6 = f32[256,256]{1,0:T(8,128)S(1)} collective-permute-done((f32[256,256]{1,0:T(8,128)S(1)}, f32[256,256]{1,0:T(8,128)S(1)}, u32[]{:S(2)}, u32[]{:S(2)}) %collective-permute-start.6) | collective-permute-done | bytes 262176 | tf_op jit(solution)/shard_map/ppermute | solution.py:43
  59.9 2.8 %collective-permute-done.9 = f32[256,256]{1,0:T(8,128)S(1)} collective-permute-done((f32[256,256]{1,0:T(8,128)S(1)}, f32[256,256]{1,0:T(8,128)S(1)}, u32[]{:S(2)}, u32[]{:S(2)}) %collective-permute-start.9) | collective-permute-done | bytes 262176 | tf_op jit(solution)/shard_map/ppermute | solution.py:43
  62.7 2.2 %collective-permute-done.8 = f32[256,256]{1,0:T(8,128)S(1)} collective-permute-done((f32[256,256]{1,0:T(8,128)S(1)}, f32[256,256]{1,0:T(8,128)S(1)}, u32[]{:S(2)}, u32[]{:S(2)}) %collective-permute-start.8) | collective-permute-done | bytes 262176 | tf_op jit(solution)/shard_map/ppermute | solution.py:43
  65.0 2.8 %collective-permute-done.11 = f32[256,256]{1,0:T(8,128)S(1)} collective-permute-done((f32[256,256]{1,0:T(8,128)S(1)}, f32[256,256]{1,0:T(8,128)S(1)}, u32[]{:S(2)}, u32[]{:S(2)}) %collective-permute-start.11) | collective-permute-done | bytes 262176 | tf_op jit(solution)/shard_map/ppermute | solution.py:43
  68.2 6.1 %collective-permute-done.15.refs_5_ = f32[256,256]{1,0:T(8,128)S(1)} collective-permute-done((f32[256,256]{1,0:T(8,128)S(1)}, f32[256,256]{1,0:T(8,128)S(1)}, u32[]{:S(2)}, u32[]{:S(2)}) %collective-permute-start.15) | collective-permute-done | bytes 262176 | tf_op jit(solution)/shard_map/ppermute | solution.py:43
  74.3 2.8 %collective-permute-start.17 = (f32[256,256]{1,0:T(8,128)S(1)}, f32[256,256]{1,0:T(8,128)S(1)}, u32[]{:S(2)}, u32[]{:S(2)}) collective-permute-start(f32[256,256]{1,0:T(8,128)S(1)} %collective-permute-done.15.refs_5_), channel_id=1, source_target_pairs={{0,79},{1,0},{2,1},{3,2},{4,3},{5,4},{6,5},{7,6},{8,7},{9,8},{10,9... | collective-permute-start | bytes 786440 | tf_op jit(solution)/shard_map/ppermute | solution.py:43
  77.2 7.7 %collective-permute-start.16 = (f32[256,256]{1,0:T(8,128)S(1)}, f32[256,256]{1,0:T(8,128)S(1)}, u32[]{:S(2)}, u32[]{:S(2)}) collective-permute-start(f32[256,256]{1,0:T(8,128)S(1)} %collective-permute-done.14.refs_4_), channel_id=1, source_target_pairs={{0,79},{1,0},{2,1},{3,2},{4,3},{5,4},{6,5},{7,6},{8,7},{9,8},{10,9... | collective-permute-start | bytes 786440 | tf_op jit(solution)/shard_map/ppermute | solution.py:43
  84.9 3.9 %collective-permute-done.16.refs_6_ = f32[256,256]{1,0:T(8,128)S(1)} collective-permute-done((f32[256,256]{1,0:T(8,128)S(1)}, f32[256,256]{1,0:T(8,128)S(1)}, u32[]{:S(2)}, u32[]{:S(2)}) %collective-permute-start.16) | collective-permute-done | bytes 262176 | tf_op jit(solution)/shard_map/ppermute | solution.py:43
  88.8 13.1 %shard_map.75 = (f32[256,256]{1,0:T(8,128)S(1)}, f32[256,256]{1,0:T(8,128)S(1)}, f32[256,256]{1,0:T(8,128)S(1)}, f32[256,256]{1,0:T(8,128)S(1)}, f32[256,256]{1,...) custom-call(s32[1,1,6,2]{3,2,1,0:T(8,128)S(1)} %copy.8.offsets_ref, ...), custom_call_target="tpu_custom_call" | custom-call | tf_op jit(solution)/shard_map/pallas_call | solution.py:257
  102.2 8.9 %collective-permute-done.19 = f32[256,256]{1,0:T(8,128)S(1)} collective-permute-done((f32[256,256]{1,0:T(8,128)S(1)}, f32[256,256]{1,0:T(8,128)S(1)}, u32[]{:S(2)}, u32[]{:S(2)}) %collective-permute-start.19) | collective-permute-done | bytes 262176 | tf_op jit(solution)/shard_map/ppermute | solution.py:43
  111.3 2.6 %collective-permute-done.22 = f32[256,256]{1,0:T(8,128)S(1)} collective-permute-done((f32[256,256]{1,0:T(8,128)S(1)}, f32[256,256]{1,0:T(8,128)S(1)}, u32[]{:S(2)}, u32[]{:S(2)}) %collective-permute-start.22) | collective-permute-done | bytes 262176 | tf_op jit(solution)/shard_map/ppermute | solution.py:43
  114.0 2.7 %collective-permute-done.18 = f32[256,256]{1,0:T(8,128)S(1)} collective-permute-done((f32[256,256]{1,0:T(8,128)S(1)}, f32[256,256]{1,0:T(8,128)S(1)}, u32[]{:S(2)}, u32[]{:S(2)}) %collective-permute-start.18) | collective-permute-done | bytes 262176 | tf_op jit(solution)/shard_map/ppermute | solution.py:43
  116.7 5.2 %collective-permute-done.20 = f32[256,256]{1,0:T(8,128)S(1)} collective-permute-done((f32[256,256]{1,0:T(8,128)S(1)}, f32[256,256]{1,0:T(8,128)S(1)}, u32[]{:S(2)}, u32[]{:S(2)}) %collective-permute-start.20) | collective-permute-done | bytes 262176 | tf_op jit(solution)/shard_map/ppermute | solution.py:43
  122.0 2.7 %collective-permute-done.23 = f32[256,256]{1,0:T(8,128)S(1)} collective-permute-done((f32[256,256]{1,0:T(8,128)S(1)}, f32[256,256]{1,0:T(8,128)S(1)}, u32[]{:S(2)}, u32[]{:S(2)}) %collective-permute-start.23) | collective-permute-done | bytes 262176 | tf_op jit(solution)/shard_map/ppermute | solution.py:43
  (47 shorter events, 8.1 us)
Async XLA Ops:
  1.1 13.4 %collective-permute-start.3 = (f32[256,256]{1,0:T(8,128)S(1)}, f32[256,256]{1,0:T(8,128)S(1)}, u32[]{:S(2)}, u32[]{:S(2)}) collective-permute-start(f32[256,256]{1,0:T(8,128)S(1)} %get-tuple-element.39), channel_id=1, source_target_pairs={{0,120},{1,121},{2,122},{3,123},{4,124},{5,125},{6,126},{7,127},{8... | collective-permute-start | bytes 786440 | tf_op jit(solution)/shard_map/ppermute | solution.py:43
  7.7 11.2 %collective-permute-start.2 = (f32[256,256]{1,0:T(8,128)S(1)}, f32[256,256]{1,0:T(8,128)S(1)}, u32[]{:S(2)}, u32[]{:S(2)}) collective-permute-start(f32[256,256]{1,0:T(8,128)S(1)} %get-tuple-element.40), channel_id=1, source_target_pairs={{0,120},{1,121},{2,122},{3,123},{4,124},{5,125},{6,126},{7,127},{8... | collective-permute-start | bytes 786440 | tf_op jit(solution)/shard_map/ppermute | solution.py:43
  8.5 23.6 %collective-permute-start.1 = (f32[256,256]{1,0:T(8,128)S(1)}, f32[256,256]{1,0:T(8,128)S(1)}, u32[]{:S(2)}, u32[]{:S(2)}) collective-permute-start(f32[256,256]{1,0:T(8,128)S(1)} %get-tuple-element.39), channel_id=1, source_target_pairs={{0,79},{1,0},{2,1},{3,2},{4,3},{5,4},{6,5},{7,6},{8,7},{9,8},{10,9... | collective-permute-start | bytes 786440 | tf_op jit(solution)/shard_map/ppermute | solution.py:43
  9.9 22.1 %collective-permute-start = (f32[256,256]{1,0:T(8,128)S(1)}, f32[256,256]{1,0:T(8,128)S(1)}, u32[]{:S(2)}, u32[]{:S(2)}) collective-permute-start(f32[256,256]{1,0:T(8,128)S(1)} %get-tuple-element.40), channel_id=1, source_target_pairs={{0,79},{1,0},{2,1},{3,2},{4,3},{5,4},{6,5},{7,6},{8,7},{9,8},{10,9... | collective-permute-start | bytes 786440 | tf_op jit(solution)/shard_map/ppermute | solution.py:43
  14.4 17.7 %collective-permute-start.5 = (f32[256,256]{1,0:T(8,128)S(1)}, f32[256,256]{1,0:T(8,128)S(1)}, u32[]{:S(2)}, u32[]{:S(2)}) collective-permute-start(f32[256,256]{1,0:T(8,128)S(1)} %collective-permute-done.3.refs_4_), channel_id=1, source_target_pairs={{0,79},{1,0},{2,1},{3,2},{4,3},{5,4},{6,5},{7,6},{8,7},{9,8},{10,9... | collective-permute-start | bytes 786440 | tf_op jit(solution)/shard_map/ppermute | solution.py:43
  18.9 13.2 %collective-permute-start.4 = (f32[256,256]{1,0:T(8,128)S(1)}, f32[256,256]{1,0:T(8,128)S(1)}, u32[]{:S(2)}, u32[]{:S(2)}) collective-permute-start(f32[256,256]{1,0:T(8,128)S(1)} %collective-permute-done.2.refs_3_), channel_id=1, source_target_pairs={{0,79},{1,0},{2,1},{3,2},{4,3},{5,4},{6,5},{7,6},{8,7},{9,8},{10,9... | collective-permute-start | bytes 786440 | tf_op jit(solution)/shard_map/ppermute | solution.py:43
  45.1 9.2 %collective-permute-start.7 = (f32[256,256]{1,0:T(8,128)S(1)}, f32[256,256]{1,0:T(8,128)S(1)}, u32[]{:S(2)}, u32[]{:S(2)}) collective-permute-start(f32[256,256]{1,0:T(8,128)S(1)} %get-tuple-element.24), channel_id=1, source_target_pairs={{0,1},{1,2},{2,3},{3,4},{4,5},{5,6},{6,7},{7,8},{8,9},{9,10},{10,1... | collective-permute-start | bytes 786440 | tf_op jit(solution)/shard_map/ppermute | solution.py:43
  45.2 11.9 %collective-permute-start.10 = (f32[256,256]{1,0:T(8,128)S(1)}, f32[256,256]{1,0:T(8,128)S(1)}, u32[]{:S(2)}, u32[]{:S(2)}) collective-permute-start(f32[256,256]{1,0:T(8,128)S(1)} %get-tuple-element.28), channel_id=1, source_target_pairs={{0,1},{1,2},{2,3},{3,4},{4,5},{5,6},{6,7},{7,8},{8,9},{9,10},{10,1... | collective-permute-start | bytes 786440 | tf_op jit(solution)/shard_map/ppermute | solution.py:43
  45.3 14.6 %collective-permute-start.6 = (f32[256,256]{1,0:T(8,128)S(1)}, f32[256,256]{1,0:T(8,128)S(1)}, u32[]{:S(2)}, u32[]{:S(2)}) collective-permute-start(f32[256,256]{1,0:T(8,128)S(1)} %get-tuple-element.22), channel_id=1, source_target_pairs={{0,1},{1,2},{2,3},{3,4},{4,5},{5,6},{6,7},{7,8},{8,9},{9,10},{10,1... | collective-permute-start | bytes 786440 | tf_op jit(solution)/shard_map/ppermute | solution.py:43
  45.4 17.4 %collective-permute-start.9 = (f32[256,256]{1,0:T(8,128)S(1)}, f32[256,256]{1,0:T(8,128)S(1)}, u32[]{:S(2)}, u32[]{:S(2)}) collective-permute-start(f32[256,256]{1,0:T(8,128)S(1)} %get-tuple-element.26), channel_id=1, source_target_pairs={{0,1},{1,2},{2,3},{3,4},{4,5},{5,6},{6,7},{7,8},{8,9},{9,10},{10,1... | collective-permute-start | bytes 786440 | tf_op jit(solution)/shard_map/ppermute | solution.py:43
  54.3 10.6 %collective-permute-start.8 = (f32[256,256]{1,0:T(8,128)S(1)}, f32[256,256]{1,0:T(8,128)S(1)}, u32[]{:S(2)}, u32[]{:S(2)}) collective-permute-start(f32[256,256]{1,0:T(8,128)S(1)} %add.37), channel_id=1, source_target_pairs={{0,16},{1,17},{2,18},{3,19},{4,20},{5,21},{6,22},{7,23},{8,24},{9,... | collective-permute-start | bytes 786440 | tf_op jit(solution)/shard_map/ppermute | solution.py:43
  57.2 10.6 %collective-permute-start.11 = (f32[256,256]{1,0:T(8,128)S(1)}, f32[256,256]{1,0:T(8,128)S(1)}, u32[]{:S(2)}, u32[]{:S(2)}) collective-permute-start(f32[256,256]{1,0:T(8,128)S(1)} %add.40), channel_id=1, source_target_pairs={{0,16},{1,17},{2,18},{3,19},{4,20},{5,21},{6,22},{7,23},{8,24},{9,... | collective-permute-start | bytes 786440 | tf_op jit(solution)/shard_map/ppermute | solution.py:43
  67.9 6.4 %collective-permute-start.15 = (f32[256,256]{1,0:T(8,128)S(1)}, f32[256,256]{1,0:T(8,128)S(1)}, u32[]{:S(2)}, u32[]{:S(2)}) collective-permute-start(f32[256,256]{1,0:T(8,128)S(1)} %get-tuple-element.38.refs_1_), channel_id=1, source_target_pairs={{0,120},{1,121},{2,122},{3,123},{4,124},{5,125},{6,126},{7,127},{8... | collective-permute-start | bytes 786440 | tf_op jit(solution)/shard_map/ppermute | solution.py:43
  68.0 9.2 %collective-permute-start.14 = (f32[256,256]{1,0:T(8,128)S(1)}, f32[256,256]{1,0:T(8,128)S(1)}, u32[]{:S(2)}, u32[]{:S(2)}) collective-permute-start(f32[256,256]{1,0:T(8,128)S(1)} %get-tuple-element.37.refs_0_), channel_id=1, source_target_pairs={{0,120},{1,121},{2,122},{3,123},{4,124},{5,125},{6,126},{7,127},{8... | collective-permute-start | bytes 786440 | tf_op jit(solution)/shard_map/ppermute | solution.py:43
  68.1 16.8 %collective-permute-start.13 = (f32[256,256]{1,0:T(8,128)S(1)}, f32[256,256]{1,0:T(8,128)S(1)}, u32[]{:S(2)}, u32[]{:S(2)}) collective-permute-start(f32[256,256]{1,0:T(8,128)S(1)} %get-tuple-element.38.refs_1_), channel_id=1, source_target_pairs={{0,79},{1,0},{2,1},{3,2},{4,3},{5,4},{6,5},{7,6},{8,7},{9,8},{10,9... | collective-permute-start | bytes 786440 | tf_op jit(solution)/shard_map/ppermute | solution.py:43
  68.2 16.7 %collective-permute-start.12 = (f32[256,256]{1,0:T(8,128)S(1)}, f32[256,256]{1,0:T(8,128)S(1)}, u32[]{:S(2)}, u32[]{:S(2)}) collective-permute-start(f32[256,256]{1,0:T(8,128)S(1)} %get-tuple-element.37.refs_0_), channel_id=1, source_target_pairs={{0,79},{1,0},{2,1},{3,2},{4,3},{5,4},{6,5},{7,6},{8,7},{9,8},{10,9... | collective-permute-start | bytes 786440 | tf_op jit(solution)/shard_map/ppermute | solution.py:43
  74.3 10.5 %collective-permute-start.17 = (f32[256,256]{1,0:T(8,128)S(1)}, f32[256,256]{1,0:T(8,128)S(1)}, u32[]{:S(2)}, u32[]{:S(2)}) collective-permute-start(f32[256,256]{1,0:T(8,128)S(1)} %collective-permute-done.15.refs_5_), channel_id=1, source_target_pairs={{0,79},{1,0},{2,1},{3,2},{4,3},{5,4},{6,5},{7,6},{8,7},{9,8},{10,9... | collective-permute-start | bytes 786440 | tf_op jit(solution)/shard_map/ppermute | solution.py:43
  77.2 11.6 %collective-permute-start.16 = (f32[256,256]{1,0:T(8,128)S(1)}, f32[256,256]{1,0:T(8,128)S(1)}, u32[]{:S(2)}, u32[]{:S(2)}) collective-permute-start(f32[256,256]{1,0:T(8,128)S(1)} %collective-permute-done.14.refs_4_), channel_id=1, source_target_pairs={{0,79},{1,0},{2,1},{3,2},{4,3},{5,4},{6,5},{7,6},{8,7},{9,8},{10,9... | collective-permute-start | bytes 786440 | tf_op jit(solution)/shard_map/ppermute | solution.py:43
  101.9 9.2 %collective-permute-start.19 = (f32[256,256]{1,0:T(8,128)S(1)}, f32[256,256]{1,0:T(8,128)S(1)}, u32[]{:S(2)}, u32[]{:S(2)}) collective-permute-start(f32[256,256]{1,0:T(8,128)S(1)} %get-tuple-element.32), channel_id=1, source_target_pairs={{0,1},{1,2},{2,3},{3,4},{4,5},{5,6},{6,7},{7,8},{8,9},{9,10},{10,1... | collective-permute-start | bytes 786440 | tf_op jit(solution)/shard_map/ppermute | solution.py:43
  102.0 11.9 %collective-permute-start.22 = (f32[256,256]{1,0:T(8,128)S(1)}, f32[256,256]{1,0:T(8,128)S(1)}, u32[]{:S(2)}, u32[]{:S(2)}) collective-permute-start(f32[256,256]{1,0:T(8,128)S(1)} %get-tuple-element.36), channel_id=1, source_target_pairs={{0,1},{1,2},{2,3},{3,4},{4,5},{5,6},{6,7},{7,8},{8,9},{9,10},{10,1... | collective-permute-start | bytes 786440 | tf_op jit(solution)/shard_map/ppermute | solution.py:43
  102.1 14.6 %collective-permute-start.18 = (f32[256,256]{1,0:T(8,128)S(1)}, f32[256,256]{1,0:T(8,128)S(1)}, u32[]{:S(2)}, u32[]{:S(2)}) collective-permute-start(f32[256,256]{1,0:T(8,128)S(1)} %get-tuple-element.30), channel_id=1, source_target_pairs={{0,1},{1,2},{2,3},{3,4},{4,5},{5,6},{6,7},{7,8},{8,9},{9,10},{10,1... | collective-permute-start | bytes 786440 | tf_op jit(solution)/shard_map/ppermute | solution.py:43
  111.1 10.8 %collective-permute-start.20 = (f32[256,256]{1,0:T(8,128)S(1)}, f32[256,256]{1,0:T(8,128)S(1)}, u32[]{:S(2)}, u32[]{:S(2)}) collective-permute-start(f32[256,256]{1,0:T(8,128)S(1)} %add.43), channel_id=1, source_target_pairs={{0,16},{1,17},{2,18},{3,19},{4,20},{5,21},{6,22},{7,23},{8,24},{9,... | collective-permute-start | bytes 786440 | tf_op jit(solution)/shard_map/ppermute | solution.py:43
  111.2 10.8 %collective-permute-start.21 = (f32[256,256]{1,0:T(8,128)S(1)}, f32[256,256]{1,0:T(8,128)S(1)}, u32[]{:S(2)}, u32[]{:S(2)}) collective-permute-start(f32[256,256]{1,0:T(8,128)S(1)} %get-tuple-element.34), channel_id=1, source_target_pairs={{0,1},{1,2},{2,3},{3,4},{4,5},{5,6},{6,7},{7,8},{8,9},{9,10},{10,1... | collective-permute-start | bytes 786440 | tf_op jit(solution)/shard_map/ppermute | solution.py:43
  114.0 10.8 %collective-permute-start.23 = (f32[256,256]{1,0:T(8,128)S(1)}, f32[256,256]{1,0:T(8,128)S(1)}, u32[]{:S(2)}, u32[]{:S(2)}) collective-permute-start(f32[256,256]{1,0:T(8,128)S(1)} %add.46), channel_id=1, source_target_pairs={{0,16},{1,17},{2,18},{3,19},{4,20},{5,21},{6,22},{7,23},{8,24},{9,... | collective-permute-start | bytes 786440 | tf_op jit(solution)/shard_map/ppermute | solution.py:43
  (5 other events, 7.9 us)
